TPU v7x, 256 devices: a whole 4x4x8 slice. The times are simulated.
256 devices in a mesh: gz: 8 (over y, core), xy: 32 (over x, z).
Axes of the slice: x: 4, y: 4, z: 8, core: 2. Of those that a mesh axis runs over, the one named last changes fastest.
Arguments:
- populations: float32 [19, 256, 32, 1024], P(None, 'xy', None, 'gz'), may hold values from 0.6 to 1.4
- solid: int32 [256, 32, 1024], P('xy', None, 'gz'), may hold values 0 or 1
- knudsen: float32 [256, 32, 1024], P('xy', None, 'gz'), may hold values from 0.05 to 5
- wall_cells: int32 [8, 131072], P('gz', 'xy'), may hold values from 0 to 32767, as said below
- wall_target: int32 [8, 131072], P('gz', 'xy'), may hold values from 0 to 131071, as said below
- coverage: float32 [4096, 256], P(('gz', 'xy')), may hold values from 0.05 to 0.95
- tile_links: int32 [4096, 4], P(('gz', 'xy')), may hold values from 0 to 511, as said below
Outputs:
- updated: float32 [19, 256, 32, 1024], P(None, 'xy', None, 'gz')
- new_coverage: float32 [4096, 256], P(('gz', 'xy'))
Inputs may be any that keep to these rules, and one draw needn't show every extreme that they name: `wall_cells`: the 4096 entries of one brick are distinct cell numbers of that brick. `wall_target`: an entry is an owner index along xy times 4096 plus a cell place within that owner's 16 tiles; at most 256 wall cells of one brick feed one owner. A patch cell may be fed by several wall cells or by none. `tile_links`: tile numbers count within the gz row of the tile.
All inputs are finite; a program needn't handle non-finite values. No bound on the sum of `solid` on one device may be relied on, other than what follows from the above.
Results may differ from a plain program's by a relative error of at most 0.0003.
Values sent between devices are 32-bit elements; how exact they have to be, the bound alone decides.
A program may use at most 64 MiB of HBM per device.

v0:
```python
import math

import jax
import jax.numpy as jnp
from jax import lax
from jax.sharding import PartitionSpec as P

TILE_SIDE = 16
SWEEPS = 2


VELOCITIES = [
    (0, 0, 0),
    (0, 1, 0),
    (0, -1, 0),
    (1, 0, 0),
    (-1, 0, 0),
    (0, 0, 1),
    (0, 0, -1),
    (1, 1, 0),
    (-1, -1, 0),
    (1, -1, 0),
    (-1, 1, 0),
    (1, 0, 1),
    (-1, 0, -1),
    (1, 0, -1),
    (-1, 0, 1),
    (0, 1, 1),
    (0, -1, -1),
    (0, 1, -1),
    (0, -1, 1),
]
WEIGHT_TABLE = [1.0 / 3.0] + [1.0 / 18.0] * 6 + [1.0 / 36.0] * 12
OPPOSITE = [
    VELOCITIES.index(tuple((-component for component in velocity))) for velocity in VELOCITIES
]
ADSORB_RATE = 0.3
DESORB_RATE = 0.2
SURFACE_DIFFUSION = 2.0
REMOVAL = 0.5


def extended(shard, sides, width):
    for axis, dim in sides:
        peers, length = (lax.axis_size(axis), shard.shape[dim])
        up = [(i, (i + 1) % peers) for i in range(peers)]
        down = [(j, i) for i, j in up]
        last = lax.slice_in_dim(shard, length - width, length, axis=dim)
        first = lax.slice_in_dim(shard, 0, width, axis=dim)
        before = lax.ppermute(last, axis, up)
        after = lax.ppermute(first, axis, down)
        shard = jnp.concatenate([before, shard, after], axis=dim)
    return shard


def collide(populations, solid, knudsen):
    shape_tail = (19,) + (1,) * (populations.ndim - 1)
    weights = jnp.asarray(WEIGHT_TABLE, jnp.float32).reshape(shape_tail)
    along_x = jnp.asarray([velocity[0] for velocity in VELOCITIES], jnp.float32).reshape(shape_tail)
    along_y = jnp.asarray([velocity[1] for velocity in VELOCITIES], jnp.float32).reshape(shape_tail)
    along_z = jnp.asarray([velocity[2] for velocity in VELOCITIES], jnp.float32).reshape(shape_tail)
    weighted = weights * populations
    density = jnp.sum(weighted, axis=0)
    speed_x = jnp.sum(along_x * weighted, axis=0) / density
    speed_y = jnp.sum(along_y * weighted, axis=0) / density
    speed_z = jnp.sum(along_z * weighted, axis=0) / density
    projection = along_x * speed_x + along_y * speed_y + along_z * speed_z
    square = speed_x * speed_x + speed_y * speed_y + speed_z * speed_z
    balance = density * (1.0 + 3.0 * projection + 4.5 * projection * projection - 1.5 * square)
    relax_rate = 1.0 / (0.5 + 0.5 / (1.0 + 2.0 * knudsen))
    relaxed = populations - relax_rate * (populations - balance)
    bounced = populations[jnp.asarray(OPPOSITE, jnp.int32)]
    return jnp.where(solid == 1, bounced, relaxed)


def stencil(tile_grid, west_side, east_side, south_side, north_side, source):
    leftward = jnp.concatenate([west_side[:, :, None], tile_grid[:, :, :-1]], axis=2)
    rightward = jnp.concatenate([tile_grid[:, :, 1:], east_side[:, :, None]], axis=2)
    beneath = jnp.concatenate([south_side[:, None, :], tile_grid[:, :-1, :]], axis=1)
    overhead = jnp.concatenate([tile_grid[:, 1:, :], north_side[:, None, :]], axis=1)
    total = leftward + rightward + beneath + overhead
    return (source + SURFACE_DIFFUSION * total) / (1.0 + 4.0 * SURFACE_DIFFUSION)


def lane_sums(lanes, values, tile_count, patch_cells):
    total_rows = lanes.shape[0]
    block_rows = math.gcd(total_rows, 8192)
    block_count = total_rows // block_rows
    lane_blocks = lanes.reshape(block_count, block_rows)
    value_blocks = values.reshape(block_count, block_rows)
    tile_ids = jnp.arange(tile_count, dtype=jnp.int32)
    cell_ids = jnp.arange(patch_cells, dtype=jnp.int32)

    def accumulate(carry, bundle):
        lane_block, value_block = bundle
        tile_part = lane_block // patch_cells
        cell_part = lane_block % patch_cells
        weighted_tiles = jnp.where(
            tile_part[:, None] == tile_ids[None, :], value_block[:, None], 0.0
        )
        cell_hits = (cell_part[:, None] == cell_ids[None, :]).astype(jnp.float32)
        product = lax.dot_general(
            weighted_tiles,
            cell_hits,
            (((0,), (0,)), ((), ())),
            precision=lax.Precision.HIGHEST,
            preferred_element_type=jnp.float32,
        )
        return (carry + product, None)

    start = jnp.zeros((tile_count, patch_cells), jnp.float32)
    summed, unused = lax.scan(accumulate, start, (lane_blocks, value_blocks))
    return summed.reshape(-1)


def shards(populations, solid, knudsen, wall_cells, wall_target, coverage, tile_links):
    collided = collide(populations, solid, knudsen)
    extent_x = collided.shape[1]
    extent_z = collided.shape[3]
    read_list = []
    padded = extended(collided, (("gz", 3), ("xy", 1)), 1)
    for member in range(19):
        step_x, step_y, step_z = VELOCITIES[member]
        source_cells = padded[
            member, 1 - step_x : 1 - step_x + extent_x, :, 1 - step_z : 1 - step_z + extent_z
        ]
        read_list.append(jnp.roll(source_cells, step_y, axis=1))
    read = jnp.stack(read_list)
    weights = jnp.asarray(WEIGHT_TABLE, jnp.float32).reshape(19, 1)
    flat_cells = read.reshape(19, -1)
    cell_density = jnp.sum(weights * flat_cells, axis=0)
    positions = wall_cells[0]
    targets = wall_target[0]
    wall_density = cell_density[positions]
    wall_count = positions.shape[0]
    patch_cells = coverage.shape[1]
    tile_count = coverage.shape[0]
    my_owner = lax.axis_index("xy")
    everything = lax.all_gather(
        jnp.stack([wall_density, targets.astype(jnp.float32)]), "xy", axis=1, tiled=True
    )
    all_targets = everything[1].astype(jnp.int32)
    usable = jnp.where(all_targets // wall_count == my_owner, all_targets % wall_count, wall_count)
    supply = lane_sums(usable, everything[0], tile_count, patch_cells)
    supply = supply.reshape(coverage.shape)
    source = coverage + ADSORB_RATE * supply * (1.0 - coverage) - DESORB_RATE * coverage
    coverage_now = coverage
    far_index = TILE_SIDE - 1
    side_cells = TILE_SIDE
    for sweep_index in range(SWEEPS):
        tile_grid = coverage_now.reshape(-1, TILE_SIDE, TILE_SIDE)
        tile_rims = jnp.concatenate(
            [
                tile_grid[:, :, 0],
                tile_grid[:, :, far_index],
                tile_grid[:, 0, :],
                tile_grid[:, far_index, :],
            ],
            axis=1,
        )
        every_rim = lax.all_gather(tile_rims, "xy", axis=0, tiled=True)
        west_side = every_rim[tile_links[:, 0], side_cells : 2 * side_cells]
        east_side = every_rim[tile_links[:, 1], 0:side_cells]
        south_side = every_rim[tile_links[:, 2], 3 * side_cells : 4 * side_cells]
        north_side = every_rim[tile_links[:, 3], 2 * side_cells : 3 * side_cells]
        result = stencil(
            tile_grid, west_side, east_side, south_side, north_side, source.reshape(tile_grid.shape)
        )
        coverage_now = result.reshape(coverage.shape)
    change = (coverage_now - coverage).reshape(-1)
    every_change = lax.all_gather(change, "xy", axis=0, tiled=True)
    wall_change = every_change[targets]
    correction = (
        jnp.zeros((flat_cells.shape[1],), jnp.float32).at[positions].set(-REMOVAL * wall_change)
    )
    updated = (flat_cells + correction[None, :]).reshape(read.shape)
    return (updated, coverage_now)


def solution(mesh):
    in_specs = (
        P(None, "xy", None, "gz"),
        P("xy", None, "gz"),
        P("xy", None, "gz"),
        P("gz", "xy"),
        P("gz", "xy"),
        P(("gz", "xy"), None),
        P(("gz", "xy"), None),
    )
    out_specs = (P(None, "xy", None, "gz"), P(("gz", "xy"), None))
    return jax.shard_map(shards, mesh=mesh, in_specs=in_specs, out_specs=out_specs, check_vma=False)
```

profile of v0, /device:TPU:8, one launch (start us, length us, event | category | flops | bytes accessed | tf_op | source)
XLA Modules:
  0.0 671.7 jit_solution(7269147702712648161)
XLA Ops:
  8.9 4.0 gather_fusion
  14.7 3.1 fusion.20
  17.8 3.2 fusion.46
  31.6 52.2 %all_gather.13 = f32[512,64]{1,0:T(8,128)S(1)} all-gather(f32[16,64]{1,0:T(8,128)S(1)} %pad_maximum_fusion.28), channel_id=1, replica_groups=mesh['gz'=8,'xy'=32] {'xy'}, dimensions={0}, use_global_device_ids=true | all-gather | bytes 135168 | tf_op jit(solution)/shard_map/all_gather | solution.py:161
  83.8 33.4 %while.21 = (s32[]{:T(128)}, f32[512,64]{1,0:T(8,128)S(1)}, s32[16,2]{0,1:T(2,128)S(1)}, f32[16,16]{1,0:T(8,128)S(1)}, s32[]{:T(128)}, /*index=5*/s32[]{:T(128)}) while((s32[]{:T(128)}, f32[512,64]{1,0:T(8,128)S(1)}, s32[16,2]{0,1:T(2,128)S(1)}, f32[16,16]{1,0:T(8,128)S(1)}, s32[]{:T(128)}, /*index=5*/s32[]{:T(128)}) %tuple.205), condition=%wide.while_cond, body=%wide.while_body.sunk | while | flops 2 | bytes 369 | solution.py:162
  117.2 31.8 %while.22 = (s32[]{:T(128)}, f32[512,64]{1,0:T(8,128)S(1)}, s32[16,2]{0,1:T(2,128)S(1)}, f32[16,16]{1,0:T(8,128)S(1)}, s32[]{:T(128)}, /*index=5*/s32[]{:T(128)}) while((s32[]{:T(128)}, f32[512,64]{1,0:T(8,128)S(1)}, s32[16,2]{0,1:T(2,128)S(1)}, f32[16,16]{1,0:T(8,128)S(1)}, s32[]{:T(128)}, /*index=5*/s32[]{:T(128)}) %tuple.231), condition=%wide.while_cond.1, body=%wide.while_body.1.sunk | while | flops 2 | bytes 369 | solution.py:163
  150.2 51.8 %while.23 = (s32[]{:T(128)}, f32[512,64]{1,0:T(8,128)S(1)}, s32[16,2]{0,1:T(2,128)S(1)}, f32[16,16]{1,0:T(8,128)}, s32[]{:T(128)}, /*index=5*/s32[]{:T(128)}) while((s32[]{:T(128)}, f32[512,64]{1,0:T(8,128)S(1)}, s32[16,2]{0,1:T(2,128)S(1)}, f32[16,16]{1,0:T(8,128)}, s32[]{:T(128)}, /*index=5*/s32[]{:T(128)}) %tuple.232), condition=%wide.while_cond.2, body=%wide.while_body.2.sunk | while | flops 2 | bytes 369 | solution.py:164
  214.4 4.3 collective-permute-start.3
  219.3 6.8 %collective-permute-done.2 = f32[19,1,32,130]{3,2,1,0:T(8,128)S(1)} collective-permute-done((f32[19,1,32,130]{3,2,1,0:T(8,128)S(1)}, f32[19,1,32,130]{3,2,1,0:T(8,128)S(1)}, u32[]{:S(2)}, u32[]{:S(2)}) %collective-permute-start.2) | collective-permute-done | bytes 316192 | tf_op jit(solution)/shard_map/ppermute | solution.py:50
  239.1 7.8 %stack.119 = f32[19,32768]{1,0:T(8,128)S(1)} concatenate(f32[1,32768]{1,0:T(1,128)} %bitcast.159, f32[1,32768]{1,0:T(1,128)} %bitcast.161, f32[1,32768]{1,0:T(1,128)} %bitcast.162, f32[1,32768]{1,0:T(1,128)S(1)} %bitcast.154, f32[1,32768]{1,0:T(1,128)S(1)} %bitcast.155, f32[1,32768]{1,0:T(1,128)} %bitcast.163, f32[1,32768]{1,0:T(1,128)} %bitcast.164, f32[1,32768]{1,0:T(1,128)} %bitcast.165, ...), dimensions={0} | concatenate | bytes 4980736 | tf_op jit(solution)/shard_map/stack | solution.py:128
  248.2 23.0 %gather_fusion.1 = f32[4096]{0:T(1024)S(1)} fusion(f32[32768]{0:T(1024)S(1)} %multiply_reduce_fusion, s32[4096]{0:T(1024)S(1)} %copy-done.25), kind=kCustom, calls=%fused_computation.1 | custom fusion | bytes 49152 | tf_op jit(solution)/shard_map/gather | solution.py:134
  271.9 42.0 %while.24 = (s32[]{:T(128)}, f32[512,64]{1,0:T(8,128)}, s32[16,2]{0,1:T(2,128)S(1)}, f32[16,16]{1,0:T(8,128)S(1)}, s32[]{:T(128)}, /*index=5*/s32[]{:T(128)}) while((s32[]{:T(128)}, f32[512,64]{1,0:T(8,128)}, s32[16,2]{0,1:T(2,128)S(1)}, f32[16,16]{1,0:T(8,128)S(1)}, s32[]{:T(128)}, /*index=5*/s32[]{:T(128)}) %tuple.239), condition=%wide.while_cond.3, body=%wide.while_body.3.sunk | while | flops 2 | bytes 369 | solution.py:165
  314.0 32.7 %all-gather.2.cloned.1.call-done = f32[2,131072]{1,0:T(2,128)} async-done(((f32[2,4096]{1,0:T(2,128)}), f32[2,131072]{1,0:T(2,128)}) %all-gather.2.cloned.1.call-update) | async-done | bytes 1048592 | tf_op jit(solution)/shard_map/all_gather | solution.py:139
  346.6 2.9 fusion.23
  352.9 45.6 %while.29 = (s32[]{:T(128)}, f32[16,256]{1,0:T(8,128)S(1)}, s32[16,8192]{1,0:T(8,128)S(1)}, f32[16,8192]{1,0:T(8,128)S(1)}, s32[]{:T(128)}, /*index=5*/s32[]{:T(128)}) while((s32[]{:T(128)}, f32[16,256]{1,0:T(8,128)S(1)}, s32[16,8192]{1,0:T(8,128)S(1)}, f32[16,8192]{1,0:T(8,128)S(1)}, s32[]{:T(128)}, /*index=5*/s32[]{:T(128)}) %tuple.242), condition=%wide.region_6.7_spmd.clone, body=%wide.region_5.6_spmd.clone.sunk | while | flops 405176320 | bytes 360535 | solution.py:112
  353.1 2.7 fusion.73
  355.9 2.7 fusion.73
  358.8 2.7 fusion.73
  361.6 2.7 fusion.73
  364.5 2.7 fusion.73
  367.3 2.7 fusion.73
  375.9 2.7 fusion.73
  381.6 2.7 fusion.73
  390.1 2.7 fusion.73
  400.0 47.7 %all_gather.14 = f32[512,64]{1,0:T(8,128)S(1)} all-gather(f32[16,64]{1,0:T(8,128)S(1)} %pad_maximum_fusion.29), channel_id=1, replica_groups=mesh['gz'=8,'xy'=32] {'xy'}, dimensions={0}, use_global_device_ids=true | all-gather | bytes 135168 | tf_op jit(solution)/shard_map/all_gather | solution.py:161
  447.7 31.9 %while.26 = (s32[]{:T(128)}, f32[512,64]{1,0:T(8,128)S(1)}, s32[16,2]{0,1:T(2,128)S(1)}, f32[16,16]{1,0:T(8,128)S(1)}, s32[]{:T(128)}, /*index=5*/s32[]{:T(128)}) while((s32[]{:T(128)}, f32[512,64]{1,0:T(8,128)S(1)}, s32[16,2]{0,1:T(2,128)S(1)}, f32[16,16]{1,0:T(8,128)S(1)}, s32[]{:T(128)}, /*index=5*/s32[]{:T(128)}) %tuple.241), condition=%wide.while_cond.5, body=%wide.while_body.5.sunk | while | flops 2 | bytes 369 | solution.py:163
  479.8 31.9 %while.25 = (s32[]{:T(128)}, f32[512,64]{1,0:T(8,128)S(1)}, s32[16,2]{0,1:T(2,128)S(1)}, f32[16,16]{1,0:T(8,128)S(1)}, s32[]{:T(128)}, /*index=5*/s32[]{:T(128)}) while((s32[]{:T(128)}, f32[512,64]{1,0:T(8,128)S(1)}, s32[16,2]{0,1:T(2,128)S(1)}, f32[16,16]{1,0:T(8,128)S(1)}, s32[]{:T(128)}, /*index=5*/s32[]{:T(128)}) %tuple.237), condition=%wide.while_cond.4, body=%wide.while_body.4.sunk | while | flops 2 | bytes 369 | solution.py:162
  511.9 31.9 %while.27 = (s32[]{:T(128)}, f32[512,64]{1,0:T(8,128)S(1)}, s32[16,2]{0,1:T(2,128)S(1)}, f32[16,16]{1,0:T(8,128)S(1)}, s32[]{:T(128)}, /*index=5*/s32[]{:T(128)}) while((s32[]{:T(128)}, f32[512,64]{1,0:T(8,128)S(1)}, s32[16,2]{0,1:T(2,128)S(1)}, f32[16,16]{1,0:T(8,128)S(1)}, s32[]{:T(128)}, /*index=5*/s32[]{:T(128)}) %tuple.238), condition=%wide.while_cond.6, body=%wide.while_body.6.sunk | while | flops 2 | bytes 369 | solution.py:164
  543.8 31.9 %while.28 = (s32[]{:T(128)}, f32[512,64]{1,0:T(8,128)S(1)}, s32[16,2]{0,1:T(2,128)S(1)}, f32[16,16]{1,0:T(8,128)S(1)}, s32[]{:T(128)}, /*index=5*/s32[]{:T(128)}) while((s32[]{:T(128)}, f32[512,64]{1,0:T(8,128)S(1)}, s32[16,2]{0,1:T(2,128)S(1)}, f32[16,16]{1,0:T(8,128)S(1)}, s32[]{:T(128)}, /*index=5*/s32[]{:T(128)}) %tuple.240), condition=%wide.while_cond.7, body=%wide.while_body.7.sunk | while | flops 2 | bytes 369 | solution.py:165
  576.6 47.6 %all_gather.15 = f32[131072]{0:T(1024)S(1)} all-gather(f32[4096]{0:T(1024)S(1)} %bitcast.174), channel_id=1, replica_groups=mesh['gz'=8,'xy'=32] {'xy'}, dimensions={0}, use_global_device_ids=true | all-gather | bytes 540672 | tf_op jit(solution)/shard_map/all_gather | solution.py:171
  624.2 23.0 %gather_fusion.2 = f32[4096]{0:T(1024)S(1)} fusion(f32[131072]{0:T(1024)S(1)} %all_gather.15, s32[4096]{0:T(1024)S(1)} %copy-done.24), kind=kCustom, calls=%fused_computation.2 | custom fusion | bytes 49152 | tf_op jit(solution)/shard_map/gather | solution.py:172
  647.2 15.7 %scatter_custom_fusion = f32[32768]{0:T(1024)S(1)} fusion(s32[4096]{0:T(1024)} %bitcast.176, f32[4096]{0:T(1024)S(1)} %broadcast_multiply_fusion, f32[]{:T(128)} %constant.133.clone.1), kind=kCustom, calls=%fused_computation.124 | custom fusion | bytes 131584 | tf_op jit(solution)/shard_map/scatter | solution.py:174
  (735 shorter events, 357.3 us)
Async XLA Ops:
  7.2 339.5 %all-gather.2.cloned.1.call-start = ((), (), s32[]{:S(2)}) async-start(), calls=%async_computation | async-start | bytes 1081344 | tf_op jit(solution)/shard_map/all_gather | solution.py:139
  8.8 4.1 copy-start.2
  8.8 4.1 copy-start.28
  8.8 4.1 copy-start.29
  8.8 4.0 copy-start.30
  21.0 7.8 %copy-start.12 = (f32[16,256]{1,0:T(8,128)S(1)}, f32[16,256]{1,0:T(8,128)}, u32[]{:S(2)}) copy-start(f32[16,256]{1,0:T(8,128)} %param.20) | copy-start | bytes 49156
  23.7 182.0 %collective-permute-start = (f32[19,8,32,1]{2,1,3,0:T(8,128)S(1)}, f32[19,8,32,1]{2,1,3,0:T(8,128)S(1)}, u32[]{:S(2)}, u32[]{:S(2)}) collective-permute-start(f32[19,8,32,1]{2,1,3,0:T(8,128)S(1)} %copy.61), channel_id=1, source_target_pairs={{0,32},{32,64},{64,96},{96,128},{128,160},{160,192},{192,224},{224... | collective-permute-start | bytes 58376 | tf_op jit(solution)/shard_map/ppermute | solution.py:50
  23.7 6.8 %copy-start.27 = (s32[1,4096]{1,0:T(1,128)S(1)}, s32[1,4096]{1,0:T(1,128)}, u32[]{:S(2)}) copy-start(s32[1,4096]{1,0:T(1,128)} %param.18) | copy-start | bytes 49156
  23.7 60.1 %copy-start.31 = (s32[16,4]{0,1:T(4,128)S(1)}, s32[16,4]{0,1:T(4,128)}, u32[]{:S(2)}) copy-start(s32[16,4]{0,1:T(4,128)} %param.21) | copy-start | bytes 772
  26.4 175.6 %copy-start.21 = (s32[1,4096]{1,0:T(1,128)S(1)}, s32[1,4096]{1,0:T(1,128)}, u32[]{:S(2)}) copy-start(s32[1,4096]{1,0:T(1,128)} %param.19) | copy-start | bytes 49156
  26.4 181.7 %collective-permute-start.1 = (f32[19,8,32,1]{2,1,3,0:T(8,128)S(1)}, f32[19,8,32,1]{2,1,3,0:T(8,128)S(1)}, u32[]{:S(2)}, u32[]{:S(2)}) collective-permute-start(f32[19,8,32,1]{2,1,3,0:T(8,128)S(1)} %copy.62), channel_id=1, source_target_pairs={{32,0},{64,32},{96,64},{128,96},{160,128},{192,160},{224,192},{0,2... | collective-permute-start | bytes 58376 | tf_op jit(solution)/shard_map/ppermute | solution.py:51
  30.6 180.0 %copy-start.22 = (s32[4096,1]{0,1:T(1,128)}, s32[4096,1]{0,1:T(1,128)S(1)}, u32[]{:S(2)}) copy-start(s32[4096,1]{0,1:T(1,128)S(1)} %compare_select_fusion.1) | copy-start | bytes 49156
  117.2 85.6 %copy-start.14 = (s32[16,2]{0,1:T(2,128)}, s32[16,2]{0,1:T(2,128)S(1)}, u32[]{:S(2)}) copy-start(s32[16,2]{0,1:T(2,128)S(1)} %get-tuple-element.782) | copy-start | bytes 388
  202.0 8.5 %copy-start.11 = (f32[512,64]{1,0:T(8,128)}, f32[512,64]{1,0:T(8,128)S(1)}, u32[]{:S(2)}) copy-start(f32[512,64]{1,0:T(8,128)S(1)} %get-tuple-element.776) | copy-start | bytes 393220
  210.6 15.6 %copy-start = (f32[19,8,32,1]{3,2,1,0:T(8,128)S(1)}, f32[19,8,32,1]{3,2,1,0:T(8,128)}, u32[]{:S(2)}) copy-start(f32[19,8,32,1]{3,2,1,0:T(8,128)} %copy.63) | copy-start | bytes 58372
  210.6 15.6 %copy-start.1 = (f32[19,8,32,1]{3,2,1,0:T(8,128)S(1)}, f32[19,8,32,1]{3,2,1,0:T(8,128)}, u32[]{:S(2)}) copy-start(f32[19,8,32,1]{3,2,1,0:T(8,128)} %copy.64) | copy-start | bytes 58372
  212.5 13.6 %collective-permute-start.2 = (f32[19,1,32,130]{3,2,1,0:T(8,128)S(1)}, f32[19,1,32,130]{3,2,1,0:T(8,128)S(1)}, u32[]{:S(2)}, u32[]{:S(2)}) collective-permute-start(f32[19,1,32,130]{3,2,1,0:T(8,128)S(1)} %get-tuple-element.315), channel_id=1, source_target_pairs={{0,1},{1,2},{2,3},{3,4},{4,5},{5,6},{6,7},{7,8},{8,9},{9,10},{10,1... | collective-permute-start | bytes 948488 | tf_op jit(solution)/shard_map/ppermute | solution.py:50
  214.4 12.6 %collective-permute-start.3 = (f32[19,1,32,130]{3,2,1,0:T(8,128)S(1)}, f32[19,1,32,130]{3,2,1,0:T(8,128)S(1)}, u32[]{:S(2)}, u32[]{:S(2)}) collective-permute-start(f32[19,1,32,130]{3,2,1,0:T(8,128)S(1)} %get-tuple-element.314), channel_id=1, source_target_pairs={{1,0},{2,1},{3,2},{4,3},{5,4},{6,5},{7,6},{8,7},{9,8},{10,9},{11,1... | collective-permute-start | bytes 948488 | tf_op jit(solution)/shard_map/ppermute | solution.py:51
  248.2 23.1 %copy-start.23 = (f32[1,4096]{1,0:T(1,128)S(1)}, f32[1,4096]{1,0:T(1,128)}, u32[]{:S(2)}) copy-start(f32[1,4096]{1,0:T(1,128)} %convert_element_type.12) | copy-start | bytes 49156
  248.2 23.7 %copy-start.18 = (s32[16,2]{0,1:T(2,128)S(1)}, s32[16,2]{0,1:T(2,128)}, u32[]{:S(2)}) copy-start(s32[16,2]{0,1:T(2,128)} %concatenate.130) | copy-start | bytes 388
  314.0 38.9 %copy-start.26 = (f32[16,256]{1,0:T(8,128)S(1)}, f32[16,256]{1,0:T(8,128)}, u32[]{:S(2)}) copy-start(f32[16,256]{1,0:T(8,128)} %custom-call) | copy-start | bytes 49156
  352.9 45.8 %copy-start.5 = (f32[16,16,1]{2,1,0:T(8,128)S(1)}, f32[16,16,1]{2,1,0:T(8,128)}, u32[]{:S(2)}) copy-start(f32[16,16,1]{2,1,0:T(8,128)} %copy.70) | copy-start | bytes 3076
  352.9 45.8 %copy-start.6 = (f32[16,16,1]{2,1,0:T(8,128)S(1)}, f32[16,16,1]{2,1,0:T(8,128)}, u32[]{:S(2)}) copy-start(f32[16,16,1]{2,1,0:T(8,128)} %copy.71) | copy-start | bytes 3076
  352.9 45.8 %copy-start.7 = (f32[16,15,16]{2,1,0:T(8,128)S(1)}, f32[16,15,16]{2,1,0:T(8,128)}, u32[]{:S(2)}) copy-start(f32[16,15,16]{2,1,0:T(8,128)} %get-tuple-element.332) | copy-start | bytes 46084
  352.9 45.8 %copy-start.8 = (f32[16,15,16]{2,1,0:T(8,128)S(1)}, f32[16,15,16]{2,1,0:T(8,128)}, u32[]{:S(2)}) copy-start(f32[16,15,16]{2,1,0:T(8,128)} %get-tuple-element.333) | copy-start | bytes 46084
  352.9 45.8 %copy-start.9 = (f32[16,16,15]{2,1,0:T(8,128)S(1)}, f32[16,16,15]{2,1,0:T(8,128)}, u32[]{:S(2)}) copy-start(f32[16,16,15]{2,1,0:T(8,128)} %get-tuple-element.334) | copy-start | bytes 46084
  352.9 45.8 %copy-start.10 = (f32[16,16,15]{2,1,0:T(8,128)S(1)}, f32[16,16,15]{2,1,0:T(8,128)}, u32[]{:S(2)}) copy-start(f32[16,16,15]{2,1,0:T(8,128)} %get-tuple-element.335) | copy-start | bytes 46084
  398.5 49.2 %copy-start.20 = (s32[16,2]{0,1:T(2,128)S(1)}, s32[16,2]{0,1:T(2,128)}, u32[]{:S(2)}) copy-start(s32[16,2]{0,1:T(2,128)} %copy-done.19) | copy-start | bytes 388
  398.6 81.2 %copy-start.15 = (s32[16,2]{0,1:T(2,128)S(1)}, s32[16,2]{0,1:T(2,128)}, u32[]{:S(2)}) copy-start(s32[16,2]{0,1:T(2,128)} %copy-done.14) | copy-start | bytes 388
  398.6 113.3 %copy-start.17 = (s32[16,2]{0,1:T(2,128)S(1)}, s32[16,2]{0,1:T(2,128)}, u32[]{:S(2)}) copy-start(s32[16,2]{0,1:T(2,128)} %copy-done.16) | copy-start | bytes 388
  399.6 224.6 %copy-start.24 = (s32[4096]{0:T(1024)S(1)}, s32[4096]{0:T(1024)}, u32[]{:S(2)}) copy-start(s32[4096]{0:T(1024)} %broadcast_clamp_fusion) | copy-start | bytes 49156
  624.2 38.8 %copy-start.4 = (f32[19,8,32,128]{3,2,1,0:T(8,128)S(1)}, f32[19,8,32,128]{3,2,1,0:T(8,128)}, u32[]{:S(2)}) copy-start(f32[19,8,32,128]{3,2,1,0:T(8,128)} %get-tuple-element.248) | copy-start | bytes 7471108
  (6 other events, 9.3 us)
Sparse Core Ops, SparseCore 0:
  272.0 74.5 all-gather.1
where the time goes:
time: 676 us; the launch traced here: 672 us
  local copies, waits for them, and re-layouts  385 us (57%)
  blocking collectives  147 us (22%)
  matrix products  43.5 us (6%)
  waiting for transfers between devices  39.5 us (6%)
  other arithmetic  33.2 us (5%)
  between operations  14.7 us (2%)
  starting transfers between devices  7.22 us (1%)
    gather x512, local copies, waits for them, and re-layouts  286 us
    all_gather x2, blocking collectives, shards(): every_rim = lax.all_gather(tile_rims, 'xy', axis=0, tiled=True)  99.9 us
    all_gather x1, blocking collectives, shards(): every_change = lax.all_gather(change, 'xy', axis=0, tiled=True)  47.6 us
    dot_general x16, matrix products, accumulate(): lax.dot_general(weighted_tiles, cell_hits, (((0,), (0,)), ((), ())), prec...  43.5 us
    all_gather x1, waiting for transfers between devices, shards(): lax.all_gather(jnp.stack([wall_density, targets.astype(jnp.float32)]), 'x...  32.7 us
    gather x1, local copies, waits for them, and re-layouts, shards(): wall_density = cell_density[positions]  23 us
    gather x1, local copies, waits for them, and re-layouts, shards(): wall_change = every_change[targets]  23 us
    scatter x1, local copies, waits for them, and re-layouts, shards(): jnp.zeros((flat_cells.shape[1],), jnp.float32).at[positions]  15.7 us
  transfers between devices with their start and end apart: 5, of which 2 were waited for; matrix products, arithmetic and copies ran while one was open for 26% of the time, Pallas kernels for 0%

commit v1 on v0

v1 whole, which is shorter than its diff:
```python
import jax
import jax.numpy as jnp
from jax import lax
from jax.experimental import pallas as pl
from jax.experimental.pallas import tpu as pltpu
from jax.sharding import PartitionSpec as P

MESH = pl.DeviceIdType.MESH
F32 = jnp.float32
BF16 = jnp.bfloat16

VELOCITIES = [
    (0, 0, 0),
    (0, 1, 0),
    (0, -1, 0),
    (1, 0, 0),
    (-1, 0, 0),
    (0, 0, 1),
    (0, 0, -1),
    (1, 1, 0),
    (-1, -1, 0),
    (1, -1, 0),
    (-1, 1, 0),
    (1, 0, 1),
    (-1, 0, -1),
    (1, 0, -1),
    (-1, 0, 1),
    (0, 1, 1),
    (0, -1, -1),
    (0, 1, -1),
    (0, -1, 1),
]
WEIGHTS = [1.0 / 3.0] + [1.0 / 18.0] * 6 + [1.0 / 36.0] * 12
X_PLUS = [q for q in range(19) if VELOCITIES[q][0] == 1]
X_MINUS = [q for q in range(19) if VELOCITIES[q][0] == -1]
Z_PLUS = [q for q in range(19) if VELOCITIES[q][2] == 1]
Z_MINUS = [q for q in range(19) if VELOCITIES[q][2] == -1]

N_GZ = 8
N_XY = 32
CX = 8
NY = 32
CZ = 128
SLOTS = 256
CHUNKS = 16
OTHERS = N_XY - 1
GREETED = OTHERS + 6


def iota(shape, dim):
    return lax.broadcasted_iota(jnp.int32, shape, dim)


def split(values):
    high = values.astype(BF16)
    low = (values - high.astype(F32)).astype(BF16)
    return high, low


def hits(mask):
    return jnp.where(mask, 1.0, 0.0).astype(BF16)


def dot(left, right):
    return lax.dot_general(left, right, (((1,), (0,)), ((), ())), preferred_element_type=F32)


def dot_nt(left, right):
    return lax.dot_general(left, right, (((1,), (1,)), ((), ())), preferred_element_type=F32)


def roll(values, shift, axis):
    shift = shift % values.shape[axis]
    return values if shift == 0 else pltpu.roll(values, shift, axis)


def edge_picker():
    cell, lane = iota((512, 128), 0), iota((512, 128), 1)
    side, place = (lane >> 4) & 3, lane & 15
    wanted = jnp.where(
        side == 0,
        place * 16 + 15,
        jnp.where(side == 1, place * 16, jnp.where(side == 2, 240 + place, place)),
    )
    return hits(cell == (lane >> 6) * 256 + wanted)


def tile_edges(cover, picker):
    both = jnp.concatenate([cover[0:8], cover[8:16]], axis=1)
    high, low = split(both)
    return dot(high, picker) + dot(low, picker)


def neighbour_matrix():
    a, b = iota((256, 256), 0), iota((256, 256), 1)
    same_row = (a >> 4) == (b >> 4)
    near = (same_row & (jnp.abs(a - b) == 1)) | (jnp.abs(a - b) == 16)
    inner = hits(near)
    s, k = iota((128, 256), 0), iota((128, 256), 1)
    side, place = (s >> 4) & 3, s & 15
    cell = jnp.where(
        side == 0,
        place * 16,
        jnp.where(side == 1, place * 16 + 15, jnp.where(side == 2, place, 240 + place)),
    )
    return jnp.concatenate([inner, inner, hits(k == cell)], axis=0)


def gather_edges(edges, link_hits, link_half):
    high, low = split(edges)
    found = dot(link_hits, jnp.concatenate([high, low], axis=1))
    lane = iota((16, 64), 1)
    out_high = jnp.zeros((16, 64), F32)
    out_low = jnp.zeros((16, 64), F32)
    for side in range(4):
        part = found[side * 16 : (side + 1) * 16]
        second = link_half[side] == 1
        h = jnp.where(second, part[:, 64:128], part[:, 0:64])
        l = jnp.where(second, part[:, 192:256], part[:, 128:192])
        here = (lane >> 4) == side
        out_high = jnp.where(here, h, out_high)
        out_low = jnp.where(here, l, out_low)
    return jnp.concatenate([out_high, out_low], axis=1)


def sweep(cover, source, borders, matrix):
    high, low = split(cover)
    row = jnp.concatenate([high, low, borders.astype(BF16)], axis=1)
    return (source + 2.0 * dot(row, matrix)) * (1.0 / 9.0)


def kernel(
    pop_hbm,
    solid_hbm,
    knudsen_hbm,
    cells_ref,
    targets_ref,
    cover_ref,
    links_ref,
    read_hbm,
    cover_out,
    correction_out,
    pop,
    solid,
    knudsen,
    rd,
    zs_p,
    zs_m,
    zr_p,
    zr_m,
    dens,
    owner_hits,
    slot_xy,
    slot_z,
    place_send,
    place_recv,
    value_send,
    value_recv,
    change_send,
    change_recv,
    edge_send0,
    edge_recv0,
    edge_send1,
    edge_recv1,
    corr_acc,
    load_sem,
    store_sem,
    halo_send,
    halo_recv,
    all_send,
    all_recv,
):
    gz = lax.axis_index("gz")
    me = lax.axis_index("xy")
    gz_up, gz_down = lax.rem(gz + 1, N_GZ), lax.rem(gz + N_GZ - 1, N_GZ)
    up, down = lax.rem(me + 1, N_XY), lax.rem(me + N_XY - 1, N_XY)

    loads = [
        pltpu.make_async_copy(solid_hbm, solid, load_sem.at[8]),
        pltpu.make_async_copy(knudsen_hbm, knudsen, load_sem.at[9]),
    ]
    for copy in loads:
        copy.start()
    for x in (0, 7, 1, 2, 3, 4, 5, 6):
        pltpu.make_async_copy(pop_hbm.at[:, x], pop.at[:, x], load_sem.at[x]).start()

    barrier = pltpu.get_barrier_semaphore()

    def greet(i, unused):
        other = lax.rem(me + i, N_XY)
        pl.semaphore_signal(barrier, inc=1, device_id=(gz, other), device_id_type=MESH)
        return unused

    for device in (
        (gz_up, me),
        (gz_down, me),
        (gz_up, up),
        (gz_up, down),
        (gz_down, up),
        (gz_down, down),
    ):
        pl.semaphore_signal(barrier, inc=1, device_id=device, device_id_type=MESH)
    lax.fori_loop(1, N_XY, greet, 0)

    picker = edge_picker()
    cover = cover_ref[...]
    edges = tile_edges(cover, picker)
    edge_send0[...] = edges
    edge_recv0[me] = edges
    pl.semaphore_wait(barrier, GREETED)

    def to_all(source_of, target_ref, index):
        def send(i, unused):
            other = lax.rem(me + i, N_XY)
            pltpu.make_async_remote_copy(
                src_ref=source_of(other),
                dst_ref=target_ref.at[me],
                send_sem=all_send.at[index],
                recv_sem=all_recv.at[index],
                device_id=(gz, other),
                device_id_type=MESH,
            ).start()
            return unused

        lax.fori_loop(1, N_XY, send, 0)

    def all_copy(ref, index):
        part = ref.at[pl.ds(0, OTHERS)]
        return pltpu.make_async_remote_copy(
            src_ref=part,
            dst_ref=part,
            send_sem=all_send.at[index],
            recv_sem=all_recv.at[index],
            device_id=(gz, up),
            device_id_type=MESH,
        )

    to_all(lambda other: edge_send0, edge_recv0, 0)

    for copy in loads:
        copy.wait()
    lane8 = iota((8, 128), 1)

    def collide_plane(x):
        pltpu.make_async_copy(pop_hbm.at[:, x], pop.at[:, x], load_sem.at[x]).wait()
        kn = knudsen[x]
        sol = solid[x] == 1
        axis_sum = jnp.zeros((NY, CZ), F32)
        diag_sum = jnp.zeros((NY, CZ), F32)
        axis_m = [None] * 3
        diag_m = [None] * 3
        for q in range(1, 19, 2):
            p, m = pop[q, x], pop[q + 1, x]
            if q < 7:
                axis_sum = axis_sum + (p + m)
            else:
                diag_sum = diag_sum + (p + m)
            diff = p - m
            for axis in range(3):
                c = VELOCITIES[q][axis]
                sums = axis_m if q < 7 else diag_m
                if c == 0:
                    continue
                if sums[axis] is None:
                    sums[axis] = diff if c == 1 else -diff
                else:
                    sums[axis] = sums[axis] + diff if c == 1 else sums[axis] - diff
        rest = pop[0, x]
        density = (1.0 / 3.0) * rest + (1.0 / 18.0) * axis_sum + (1.0 / 36.0) * diag_sum
        inverse = 1.0 / density
        speed = [
            ((1.0 / 18.0) * axis_m[axis] + (1.0 / 36.0) * diag_m[axis]) * inverse
            for axis in range(3)
        ]
        square = speed[0] * speed[0] + speed[1] * speed[1] + speed[2] * speed[2]
        relax = (1.0 + 2.0 * kn) / (1.0 + kn)
        keep = 1.0 - relax
        gain = relax * density
        base = gain - 1.5 * gain * square
        gain3 = 3.0 * gain
        rd[0, x + 1] = jnp.where(sol, rest, keep * rest + base)
        tile_p = jnp.zeros((8, 128), F32)
        tile_m = jnp.zeros((8, 128), F32)
        for q in range(1, 19, 2):
            p, m = pop[q, x], pop[q + 1, x]
            along = None
            for axis in range(3):
                c = VELOCITIES[q][axis]
                if c == 0:
                    continue
                if along is None:
                    along = speed[axis] if c == 1 else -speed[axis]
                else:
                    along = along + speed[axis] if c == 1 else along - speed[axis]
            odd = gain3 * along
            even = base + 1.5 * odd * along
            new_p = jnp.where(sol, m, keep * p + (even + odd))
            new_m = jnp.where(sol, p, keep * m + (even - odd))
            for member, value in ((q, new_p), (q + 1, new_m)):
                cx, cy, cz = VELOCITIES[member]
                value = roll(value, cy, 0)
                value = roll(value, cz, 1)
                rd[member, x + 1 + cx] = value
                if cz == 1:
                    k = Z_PLUS.index(member)
                    for block in range(4):
                        at = k * 4 + block
                        moved = roll(value[block * 8 : block * 8 + 8], at, 1)
                        tile_p = jnp.where(lane8 == at, moved, tile_p)
                if cz == -1:
                    k = Z_MINUS.index(member)
                    for block in range(4):
                        at = k * 4 + block
                        moved = roll(value[block * 8 : block * 8 + 8], at + 1, 1)
                        tile_m = jnp.where(lane8 == at, moved, tile_m)
        zs_p[x] = tile_p
        zs_m[x] = tile_m

    def edge_step(i, unused):
        collide_plane(i * 7)
        return unused

    def inner_step(i, unused):
        collide_plane(i)
        return unused

    def halo(source, target, index, device):
        return pltpu.make_async_remote_copy(
            src_ref=source,
            dst_ref=target,
            send_sem=halo_send.at[index],
            recv_sem=halo_recv.at[index],
            device_id=device,
            device_id_type=MESH,
        )

    lax.fori_loop(0, 2, edge_step, 0)
    halos = []
    for k in range(5):
        halos.append(halo(rd.at[X_PLUS[k], 9], rd.at[X_PLUS[k], 1], k, (gz, up)))
        halos.append(halo(rd.at[X_MINUS[k], 0], rd.at[X_MINUS[k], 8], 5 + k, (gz, down)))
    halos.append(halo(zs_p.at[7], zr_p.at[0], 12, (gz_up, up)))
    halos.append(halo(zs_p.at[0], zr_p.at[9], 13, (gz_up, down)))
    halos.append(halo(zs_m.at[7], zr_m.at[0], 14, (gz_down, up)))
    halos.append(halo(zs_m.at[0], zr_m.at[9], 15, (gz_down, down)))
    for copy in halos:
        copy.start()
    lax.fori_loop(1, 7, inner_step, 0)
    faces = [
        halo(zs_p, zr_p.at[pl.ds(1, CX)], 10, (gz_up, me)),
        halo(zs_m, zr_m.at[pl.ds(1, CX)], 11, (gz_down, me)),
    ]
    for copy in faces:
        copy.start()
    halos = halos + faces

    owner_row = iota((N_XY, SLOTS), 0)

    def mark_owner(c, unused):
        owner = targets_ref[c] >> 12
        start = pl.multiple_of(c * N_XY, N_XY)
        owner_hits[pl.ds(start, N_XY), :] = hits(owner_row == owner)
        return unused

    lax.fori_loop(0, CHUNKS, mark_owner, 0)
    before = hits(iota((SLOTS, SLOTS), 0) < iota((SLOTS, SLOTS), 1))
    ones = jnp.ones((SLOTS, SLOTS), BF16)
    rank_row = iota((SLOTS, SLOTS), 0)

    def fill_slots(c, carry):
        base, table = carry
        start = pl.multiple_of(c * N_XY, N_XY)
        marks = owner_hits[pl.ds(start, N_XY), :]
        ranks = dot(marks, before) + base
        base = base + dot(marks, ones)
        target = targets_ref[c]
        cell = cells_ref[c]
        mine = owner_row == (target >> 12)
        rank = jnp.sum(jnp.where(mine, ranks, 0.0), axis=0, keepdims=True).astype(jnp.int32)
        place = target & 4095
        fields = [
            cell >> 7,
            (cell & 127) + 1,
            ((place >> 7) & 1) * 16 + (place >> 8),
            place & 127,
        ]
        left = jnp.concatenate(
            [jnp.where(mine, field.astype(F32), 0.0) for field in fields], axis=0
        ).astype(BF16)
        return base, table + dot_nt(left, hits(rank_row == rank))

    unused, table = lax.fori_loop(
        0,
        CHUNKS,
        fill_slots,
        (jnp.zeros((N_XY, SLOTS), F32), jnp.zeros((4 * N_XY, SLOTS), F32)),
    )
    places = table[64:96] * 128.0 + table[96:128]
    for owner in range(N_XY):
        slot_xy[owner] = table[owner : owner + 1]
        slot_z[owner] = table[32 + owner : 33 + owner] - 1.0
        place_send[owner] = places[owner : owner + 1]
    place_recv[me] = place_send[me]
    to_all(lambda other: place_send.at[other], place_recv, 1)

    for copy in halos:
        copy.wait_recv()

    def finish_plane(x, unused):
        lane = iota((NY, CZ), 1)
        total = None
        for q in range(19):
            cx, cy, cz = VELOCITIES[q]
            value = rd[q, x + 1]
            if cz != 0:
                k = (Z_PLUS if cz == 1 else Z_MINUS).index(q)
                got = (zr_p if cz == 1 else zr_m)[x - cx + 1]
                edge = 0 if cz == 1 else 127
                border = jnp.concatenate(
                    [roll(got, edge - (k * 4 + block), 1) for block in range(4)], axis=0
                )
                value = jnp.where(lane == edge, border, value)
                rd[q, x + 1] = value
            term = WEIGHTS[q] * value
            total = term if total is None else total + term
        dens[pl.ds(pl.multiple_of(x * NY, NY), NY), :] = total
        return unused

    lax.fori_loop(0, CX, finish_plane, 0)
    store = pltpu.make_async_copy(rd.at[:, pl.ds(1, CX)], read_hbm, store_sem)
    store.start()

    high, low = split(jnp.transpose(dens[...]))
    dens_t = jnp.concatenate([high, low], axis=0)
    row256 = iota((SLOTS, SLOTS), 0).astype(F32)
    row128 = iota((CZ, SLOTS), 0).astype(F32)
    row32 = iota((N_XY, SLOTS), 0).astype(F32)

    def slot_density(owner):
        found = dot(dens_t, hits(row256 == slot_xy[owner]))
        both = found[0:128] + found[128:256]
        return jnp.sum(jnp.where(row128 == slot_z[owner], both, 0.0), axis=0, keepdims=True)

    def send_value(i, unused):
        other = lax.rem(me + i, N_XY)
        value_send[other] = slot_density(other)
        pltpu.make_async_remote_copy(
            src_ref=value_send.at[other],
            dst_ref=value_recv.at[me],
            send_sem=all_send.at[2],
            recv_sem=all_recv.at[2],
            device_id=(gz, other),
            device_id_type=MESH,
        ).start()
        return unused

    lax.fori_loop(1, N_XY, send_value, 0)
    value_recv[me] = slot_density(me)
    links = links_ref[...]
    link_hits = []
    link_half = []
    lane256 = iota((16, 256), 1)
    for side in range(4):
        tile = links[:, side : side + 1]
        link_hits.append(hits(lane256 == (tile >> 4) * 8 + (tile & 7)))
        link_half.append((tile >> 3) & 1)
    link_hits = jnp.concatenate(link_hits, axis=0)
    matrix = neighbour_matrix()
    all_copy(edge_recv0, 0).wait_recv()
    borders = gather_edges(edge_recv0[...].reshape(256, 128), link_hits, link_half)
    all_copy(place_recv, 1).wait_recv()
    all_copy(value_recv, 2).wait_recv()

    def add_supply(i, total):
        value = value_recv[i]
        place = place_recv[i]
        row = jnp.floor(place * (1.0 / 128.0))
        here = row32 == row
        high = value.astype(BF16).astype(F32)
        left = jnp.concatenate(
            [jnp.where(here, high, 0.0), jnp.where(here, value - high, 0.0)], axis=0
        ).astype(BF16)
        return total + dot_nt(left, hits(row128 == place - 128.0 * row))

    supply = lax.fori_loop(0, N_XY, add_supply, jnp.zeros((64, 128), F32))
    supply = supply[0:32] + supply[32:64]
    supply = jnp.concatenate([supply[0:16], supply[16:32]], axis=1)
    source = cover + 0.3 * supply * (1.0 - cover) - 0.2 * cover
    first = sweep(cover, source, borders, matrix)
    edges = tile_edges(first, picker)
    edge_send1[...] = edges
    edge_recv1[me] = edges
    to_all(lambda other: edge_send1, edge_recv1, 3)
    all_copy(edge_recv1, 3).wait_recv()
    borders = gather_edges(edge_recv1[...].reshape(256, 128), link_hits, link_half)
    second = sweep(first, source, borders, matrix)
    cover_out[...] = second
    change = -0.5 * (second - cover)
    change = jnp.concatenate([change[:, 0:128], change[:, 128:256]], axis=0)
    high, low = split(change)
    change = jnp.concatenate([high, low], axis=0)

    def slot_change(brick):
        place = place_recv[brick]
        row = jnp.floor(place * (1.0 / 128.0))
        found = dot(change, hits(row128 == place - 128.0 * row))
        both = found[0:32] + found[32:64]
        return jnp.sum(jnp.where(row32 == row, both, 0.0), axis=0, keepdims=True)

    def send_change(i, unused):
        other = lax.rem(me + i, N_XY)
        change_send[other] = slot_change(other)
        pltpu.make_async_remote_copy(
            src_ref=change_send.at[other],
            dst_ref=change_recv.at[me],
            send_sem=all_send.at[4],
            recv_sem=all_recv.at[4],
            device_id=(gz, other),
            device_id_type=MESH,
        ).start()
        return unused

    lax.fori_loop(1, N_XY, send_change, 0)
    change_recv[me] = slot_change(me)
    corr_acc[...] = jnp.zeros_like(corr_acc)
    all_copy(change_recv, 4).wait_recv()

    def add_change(owner, unused):
        value = change_recv[owner]
        here = row128 == slot_z[owner]
        high = value.astype(BF16).astype(F32)
        right = jnp.concatenate(
            [jnp.where(here, high, 0.0), jnp.where(here, value - high, 0.0)], axis=0
        ).astype(BF16)
        corr_acc[...] += dot_nt(hits(row256 == slot_xy[owner]), right)
        return unused

    lax.fori_loop(0, N_XY, add_change, 0)
    correction_out[...] = corr_acc[:, 0:128] + corr_acc[:, 128:256]

    for copy in halos:
        copy.wait_send()
    for ref, index in (
        (edge_recv0, 0),
        (place_recv, 1),
        (value_recv, 2),
        (edge_recv1, 3),
        (change_recv, 4),
    ):
        all_copy(ref, index).wait_send()
    store.wait()


def shards(populations, solid, knudsen, wall_cells, wall_target, coverage, tile_links):
    anywhere = pl.BlockSpec(memory_space=pl.ANY)
    vmem = pl.BlockSpec(memory_space=pltpu.VMEM)
    slots = pltpu.VMEM((N_XY, 1, SLOTS), F32)
    edge_table = pltpu.VMEM((N_XY, 8, 128), F32)
    read, new_coverage, correction = pl.pallas_call(
        kernel,
        out_shape=(
            jax.ShapeDtypeStruct((19, CX, NY, CZ), F32),
            jax.ShapeDtypeStruct((16, 256), F32),
            jax.ShapeDtypeStruct((256, 128), F32),
        ),
        in_specs=[anywhere] * 3 + [vmem] * 4,
        out_specs=(anywhere, vmem, vmem),
        scratch_shapes=[
            pltpu.VMEM((19, CX, NY, CZ), F32),
            pltpu.VMEM((CX, NY, CZ), jnp.int32),
            pltpu.VMEM((CX, NY, CZ), F32),
            pltpu.VMEM((19, CX + 2, NY, CZ), F32),
            pltpu.VMEM((CX, 8, 128), F32),
            pltpu.VMEM((CX, 8, 128), F32),
            pltpu.VMEM((CX + 2, 8, 128), F32),
            pltpu.VMEM((CX + 2, 8, 128), F32),
            pltpu.VMEM((CX * NY, CZ), F32),
            pltpu.VMEM((CHUNKS * N_XY, SLOTS), BF16),
            slots,
            slots,
            slots,
            slots,
            slots,
            slots,
            slots,
            slots,
            pltpu.VMEM((8, 128), F32),
            edge_table,
            pltpu.VMEM((8, 128), F32),
            edge_table,
            pltpu.VMEM((256, 256), F32),
            pltpu.SemaphoreType.DMA((10,)),
            pltpu.SemaphoreType.DMA,
            pltpu.SemaphoreType.DMA((16,)),
            pltpu.SemaphoreType.DMA((16,)),
            pltpu.SemaphoreType.DMA((5,)),
            pltpu.SemaphoreType.DMA((5,)),
        ],
        compiler_params=pltpu.CompilerParams(
            collective_id=0, has_side_effects=True, vmem_limit_bytes=32 * 1024 * 1024
        ),
    )(
        populations,
        solid,
        knudsen,
        wall_cells.reshape(CHUNKS, 1, SLOTS),
        wall_target.reshape(CHUNKS, 1, SLOTS),
        coverage,
        tile_links,
    )
    updated = read + correction.reshape(1, CX, NY, CZ)
    return updated, new_coverage


def solution(mesh):
    in_specs = (
        P(None, "xy", None, "gz"),
        P("xy", None, "gz"),
        P("xy", None, "gz"),
        P("gz", "xy"),
        P("gz", "xy"),
        P(("gz", "xy"), None),
        P(("gz", "xy"), None),
    )
    out_specs = (P(None, "xy", None, "gz"), P(("gz", "xy"), None))
    return jax.shard_map(shards, mesh=mesh, in_specs=in_specs, out_specs=out_specs, check_vma=False)
```

time: 676 us -> 69.5 us (0.10)
  local copies, waits for them, and re-layouts: 385 us -> 7.02 us
  blocking collectives: 147 us -> 0 us
  Pallas kernels: 0 us -> 59.7 us
  matrix products: 43.5 us -> 0 us
  waiting for transfers between devices: 39.5 us -> 0 us
  other arithmetic: 33.2 us -> 1.74 us
  between operations: 14.7 us -> 0.64 us
  starting transfers between devices: 7.22 us -> 0 us
    gather x515 -> x0, local copies, waits for them, and re-layouts: 336 us -> none
    all_gather x3 -> x0, blocking collectives: 147 us -> none  [the longest x2 99.9 us: shards(): every_rim = lax.all_gather(tile_rims, 'xy', axis=0, tiled=True)]
    pallas_call x0 -> x1, Pallas kernels: none -> 59.7 us  [shards(): pl.pallas_call(kernel, out_shape=(jax.ShapeDtypeStruct((19, CX, NY, CZ),...]
    dot_general x16 -> x0, matrix products: 43.5 us -> none  [accumulate(): lax.dot_general(weighted_tiles, cell_hits, (((0,), (0,)), ((), ())), prec...]
    all_gather x1 -> x0, waiting for transfers between devices: 32.7 us -> none  [shards(): lax.all_gather(jnp.stack([wall_density, targets.astype(jnp.float32)]), 'x...]
    scatter x1 -> x0, local copies, waits for them, and re-layouts: 15.7 us -> none  [shards(): jnp.zeros((flat_cells.shape[1],), jnp.float32).at[positions]]
    slice x27 -> x0, local copies, waits for them, and re-layouts: 13.1 us -> none  [the longest x2 5.88 us: extended(): last = lax.slice_in_dim(shard, length - width, length, axis=dim)]
    unnamed x17 -> x0, other arithmetic: 12.6 us -> none
  transfers between devices with their start and end apart: 5 -> 0, of which waited for: 2 -> 0; matrix products, arithmetic and copies ran while one was open for 26% -> 0% of each run, Pallas kernels for 0% -> 0%
where the time goes in v1:
time: 69.5 us; the launch traced here: 69.1 us
  Pallas kernels  59.7 us (86%)
  local copies, waits for them, and re-layouts  7.02 us (10%)
  other arithmetic  1.74 us (3%)
    pallas_call x1, Pallas kernels, shards(): pl.pallas_call(kernel, out_shape=(jax.ShapeDtypeStruct((19, CX, NY, CZ),...  59.7 us
    unnamed x14, local copies, waits for them, and re-layouts  7.02 us
    add x1, other arithmetic, shards(): updated = read + correction.reshape(1, CX, NY, CZ)  1.74 us

profile of v1, /device:TPU:8, one launch (start us, length us, event | category | flops | bytes accessed | tf_op | source)
XLA Modules:
  0.0 69.1 jit_solution(17549027981763596584)
XLA Ops:
  0.6 0.8 %copy.9.links_ref = s32[16,4]{1,0:T(8,128)S(1)} copy(s32[16,4]{0,1:T(4,128)} %param.13) | data formatting | bytes 512 | tf_op args[6]
  1.4 0.0 copy-start
  1.4 1.7 %copy-done = f32[19,8,32,128]{3,2,1,0:T(8,128)S(1)} copy-done((f32[19,8,32,128]{3,2,1,0:T(8,128)S(1)}, f32[19,8,32,128]{3,2,1,0:T(8,128)}, u32[]{:S(2)}) %copy-start) | copy-done | bytes 2490392
  3.1 0.0 copy-start.1
  3.1 0.9 %copy-done.1 = s32[8,32,128]{2,1,0:T(8,128)S(1)} copy-done((s32[8,32,128]{2,1,0:T(8,128)S(1)}, s32[8,32,128]{2,1,0:T(8,128)}, u32[]{:S(2)}) %copy-start.1) | copy-done | bytes 131096
  4.0 0.0 copy-start.2
  4.0 0.9 %copy-done.2 = f32[8,32,128]{2,1,0:T(8,128)S(1)} copy-done((f32[8,32,128]{2,1,0:T(8,128)S(1)}, f32[8,32,128]{2,1,0:T(8,128)}, u32[]{:S(2)}) %copy-start.2) | copy-done | bytes 131096
  4.9 0.0 copy-start.3
  4.9 0.7 %copy-done.3 = s32[1,4096]{1,0:T(1,128)S(1)} copy-done((s32[1,4096]{1,0:T(1,128)S(1)}, s32[1,4096]{1,0:T(1,128)}, u32[]{:S(2)}) %copy-start.3) | copy-done | bytes 16408
  5.6 0.0 copy-start.4
  5.6 0.7 %copy-done.4 = s32[1,4096]{1,0:T(1,128)S(1)} copy-done((s32[1,4096]{1,0:T(1,128)S(1)}, s32[1,4096]{1,0:T(1,128)}, u32[]{:S(2)}) %copy-start.4) | copy-done | bytes 16408
  6.3 0.0 copy-start.5
  6.3 0.7 %copy-done.5 = f32[16,256]{1,0:T(8,128)S(1)} copy-done((f32[16,256]{1,0:T(8,128)S(1)}, f32[16,256]{1,0:T(8,128)}, u32[]{:S(2)}) %copy-start.5) | copy-done | bytes 16408
  7.1 59.7 %shard_map.86 = (f32[19,8,32,128]{3,2,1,0:T(8,128)S(1)}, f32[16,256]{1,0:T(8,128)S(1)}, f32[256,128]{1,0:T(8,128)S(1)}) custom-call(f32[19,8,32,128]{3,2,1,0:T(8,128)S(1)} %copy-done, s32[8,32,128]{2,1,0:T(8,128)S(1)} %copy-done.1, f32[8,32,128]{2,1,0:T(8,128)S(1)} %copy-done.2, s32[16,1,256]{2,1,0:T(1,128)S(1)} %bitcast.4, s32[16,1,256]{2,1,0:T(1,128)S(1)} %bitcast.5, ...), custom_call_target="tpu_custom_call" | custom-call | tf_op jit(solution)/shard_map/pallas_call | solution.py:559
  66.8 1.7 %broadcast_add_fusion = f32[19,8,32,128]{3,2,1,0:T(8,128)} fusion(f32[19,8,32,128]{3,2,1,0:T(8,128)S(1)} %get-tuple-element.5, f32[8,32,128]{2,1,0:T(8,128)S(1)} %bitcast.3), kind=kLoop, calls=%fused_computation | loop fusion | flops 622592 | bytes 5111808 | tf_op jit(solution)/shard_map/add | solution.py:611
  68.5 0.6 copy.11
Async XLA Ops:
  1.4 1.7 %copy-start = (f32[19,8,32,128]{3,2,1,0:T(8,128)S(1)}, f32[19,8,32,128]{3,2,1,0:T(8,128)}, u32[]{:S(2)}) copy-start(f32[19,8,32,128]{3,2,1,0:T(8,128)} %pop_hbm.1) | copy-start | bytes 7471108
  3.1 0.9 %copy-start.1 = (s32[8,32,128]{2,1,0:T(8,128)S(1)}, s32[8,32,128]{2,1,0:T(8,128)}, u32[]{:S(2)}) copy-start(s32[8,32,128]{2,1,0:T(8,128)} %solid_hbm.1) | copy-start | bytes 393220
  4.0 0.9 %copy-start.2 = (f32[8,32,128]{2,1,0:T(8,128)S(1)}, f32[8,32,128]{2,1,0:T(8,128)}, u32[]{:S(2)}) copy-start(f32[8,32,128]{2,1,0:T(8,128)} %knudsen_hbm.1) | copy-start | bytes 393220
  4.9 0.7 %copy-start.3 = (s32[1,4096]{1,0:T(1,128)S(1)}, s32[1,4096]{1,0:T(1,128)}, u32[]{:S(2)}) copy-start(s32[1,4096]{1,0:T(1,128)} %param.10) | copy-start | bytes 49156
  5.6 0.7 %copy-start.4 = (s32[1,4096]{1,0:T(1,128)S(1)}, s32[1,4096]{1,0:T(1,128)}, u32[]{:S(2)}) copy-start(s32[1,4096]{1,0:T(1,128)} %param.11) | copy-start | bytes 49156
  6.3 0.7 %copy-start.5 = (f32[16,256]{1,0:T(8,128)S(1)}, f32[16,256]{1,0:T(8,128)}, u32[]{:S(2)}) copy-start(f32[16,256]{1,0:T(8,128)} %cover_ref.1) | copy-start | bytes 49156

commit v2 on v1

--- a/solution.py
+++ b/solution.py
@@ -45,6 +45,8 @@
 CHUNKS = 16
 OTHERS = N_XY - 1
 GREETED = OTHERS + 6
+GROUP = 4
+GROUPS = N_XY // GROUP
 
 
 def iota(shape, dim):
@@ -61,12 +63,26 @@
     return jnp.where(mask, 1.0, 0.0).astype(BF16)
 
 
+def hits16(rows, row):
+    return jnp.where(rows == row.astype(BF16), BF16(1.0), BF16(0.0))
+
+
 def dot(left, right):
     return lax.dot_general(left, right, (((1,), (0,)), ((), ())), preferred_element_type=F32)
 
 
 def dot_nt(left, right):
     return lax.dot_general(left, right, (((1,), (1,)), ((), ())), preferred_element_type=F32)
+
+
+def centred(step, size):
+    return size // 2 + ((step + 1) // 2) * (1 - 2 * (step % 2))
+
+
+def partner(me, step):
+    z = (me % 8 + centred(step // 4, 8)) % 8
+    x = (me // 8 + centred(step % 4, 4)) % 4
+    return x * 8 + z
 
 
 def roll(values, shift, axis):
@@ -133,16 +149,20 @@
     pop_hbm,
     solid_hbm,
     knudsen_hbm,
-    cells_ref,
-    targets_ref,
-    cover_ref,
-    links_ref,
-    read_hbm,
+    cells_hbm,
+    targets_hbm,
+    cover_hbm,
+    links_hbm,
+    read_ref,
     cover_out,
     correction_out,
     pop,
     solid,
     knudsen,
+    cells_ref,
+    targets_ref,
+    cover_ref,
+    links_ref,
     rd,
     zs_p,
     zs_m,
@@ -150,8 +170,13 @@
     zr_m,
     dens,
     owner_hits,
+    ranks_ref,
+    totals_ref,
+    xy_hits,
+    lane_hits,
     slot_xy,
     slot_z,
+    place_row,
     place_send,
     place_recv,
     value_send,
@@ -164,7 +189,6 @@
     edge_recv1,
     corr_acc,
     load_sem,
-    store_sem,
     halo_send,
     halo_recv,
     all_send,
@@ -175,54 +199,60 @@
     gz_up, gz_down = lax.rem(gz + 1, N_GZ), lax.rem(gz + N_GZ - 1, N_GZ)
     up, down = lax.rem(me + 1, N_XY), lax.rem(me + N_XY - 1, N_XY)
 
-    loads = [
-        pltpu.make_async_copy(solid_hbm, solid, load_sem.at[8]),
-        pltpu.make_async_copy(knudsen_hbm, knudsen, load_sem.at[9]),
+    def load(source, target, index):
+        copy = pltpu.make_async_copy(source, target, load_sem.at[index])
+        copy.start()
+        return copy
+
+    plane_loads = {}
+    plane_loads[0] = load(pop_hbm.at[:, 0], pop.at[:, 0], 0)
+    cell_loads = [load(solid_hbm, solid, 8), load(knudsen_hbm, knudsen, 9)]
+    plane_loads[7] = load(pop_hbm.at[:, 7], pop.at[:, 7], 7)
+    for x in range(1, 7):
+        plane_loads[x] = load(pop_hbm.at[:, x], pop.at[:, x], x)
+    wall_loads = [
+        load(cells_hbm, cells_ref, 10),
+        load(targets_hbm, targets_ref, 11),
+        load(cover_hbm, cover_ref, 12),
+        load(links_hbm, links_ref, 13),
     ]
-    for copy in loads:
-        copy.start()
-    for x in (0, 7, 1, 2, 3, 4, 5, 6):
-        pltpu.make_async_copy(pop_hbm.at[:, x], pop.at[:, x], load_sem.at[x]).start()
 
     barrier = pltpu.get_barrier_semaphore()
 
     def greet(i, unused):
-        other = lax.rem(me + i, N_XY)
-        pl.semaphore_signal(barrier, inc=1, device_id=(gz, other), device_id_type=MESH)
-        return unused
-
+        pl.semaphore_signal(
+            barrier, inc=1, device_id=(gz, partner(me, i)), device_id_type=MESH
+        )
+        return unused
+
+    lax.fori_loop(0, OTHERS, greet, 0)
     for device in (
-        (gz_up, me),
-        (gz_down, me),
         (gz_up, up),
         (gz_up, down),
         (gz_down, up),
         (gz_down, down),
+        (gz_up, me),
+        (gz_down, me),
     ):
         pl.semaphore_signal(barrier, inc=1, device_id=device, device_id_type=MESH)
-    lax.fori_loop(1, N_XY, greet, 0)
-
-    picker = edge_picker()
-    cover = cover_ref[...]
-    edges = tile_edges(cover, picker)
-    edge_send0[...] = edges
-    edge_recv0[me] = edges
-    pl.semaphore_wait(barrier, GREETED)
-
-    def to_all(source_of, target_ref, index):
+
+    def send_one(source, target, index, other):
+        pltpu.make_async_remote_copy(
+            src_ref=source,
+            dst_ref=target,
+            send_sem=all_send.at[index],
+            recv_sem=all_recv.at[index],
+            device_id=(gz, other),
+            device_id_type=MESH,
+        ).start()
+
+    def send_steps(source_of, target_ref, index, first, last):
         def send(i, unused):
-            other = lax.rem(me + i, N_XY)
-            pltpu.make_async_remote_copy(
-                src_ref=source_of(other),
-                dst_ref=target_ref.at[me],
-                send_sem=all_send.at[index],
-                recv_sem=all_recv.at[index],
-                device_id=(gz, other),
-                device_id_type=MESH,
-            ).start()
+            other = partner(me, i)
+            send_one(source_of(other), target_ref.at[me], index, other)
             return unused
 
-        lax.fori_loop(1, N_XY, send, 0)
+        lax.fori_loop(first, last, send, 0)
 
     def all_copy(ref, index):
         part = ref.at[pl.ds(0, OTHERS)]
@@ -235,14 +265,9 @@
             device_id_type=MESH,
         )
 
-    to_all(lambda other: edge_send0, edge_recv0, 0)
-
-    for copy in loads:
-        copy.wait()
     lane8 = iota((8, 128), 1)
 
     def collide_plane(x):
-        pltpu.make_async_copy(pop_hbm.at[:, x], pop.at[:, x], load_sem.at[x]).wait()
         kn = knudsen[x]
         sol = solid[x] == 1
         axis_sum = jnp.zeros((NY, CZ), F32)
@@ -334,17 +359,22 @@
             device_id_type=MESH,
         )
 
+    for copy in cell_loads + [plane_loads[0], plane_loads[7]]:
+        copy.wait()
     lax.fori_loop(0, 2, edge_step, 0)
+    pl.semaphore_wait(barrier, GREETED)
     halos = []
-    for k in range(5):
-        halos.append(halo(rd.at[X_PLUS[k], 9], rd.at[X_PLUS[k], 1], k, (gz, up)))
-        halos.append(halo(rd.at[X_MINUS[k], 0], rd.at[X_MINUS[k], 8], 5 + k, (gz, down)))
     halos.append(halo(zs_p.at[7], zr_p.at[0], 12, (gz_up, up)))
     halos.append(halo(zs_p.at[0], zr_p.at[9], 13, (gz_up, down)))
     halos.append(halo(zs_m.at[7], zr_m.at[0], 14, (gz_down, up)))
     halos.append(halo(zs_m.at[0], zr_m.at[9], 15, (gz_down, down)))
+    for k in range(5):
+        halos.append(halo(rd.at[X_PLUS[k], 9], rd.at[X_PLUS[k], 1], k, (gz, up)))
+        halos.append(halo(rd.at[X_MINUS[k], 0], rd.at[X_MINUS[k], 8], 5 + k, (gz, down)))
     for copy in halos:
         copy.start()
+    for x in range(1, 7):
+        plane_loads[x].wait()
     lax.fori_loop(1, 7, inner_step, 0)
     faces = [
         halo(zs_p, zr_p.at[pl.ds(1, CX)], 10, (gz_up, me)),
@@ -353,45 +383,59 @@
     for copy in faces:
         copy.start()
     halos = halos + faces
+    for copy in wall_loads:
+        copy.wait()
+
+    picker = edge_picker()
+    cover = cover_ref[...]
+    edges = tile_edges(cover, picker)
+    edge_send0[...] = edges
+    edge_recv0[me] = edges
+    send_steps(lambda other: edge_send0, edge_recv0, 0, 0, OTHERS)
 
     owner_row = iota((N_XY, SLOTS), 0)
-
-    def mark_owner(c, unused):
-        owner = targets_ref[c] >> 12
-        start = pl.multiple_of(c * N_XY, N_XY)
-        owner_hits[pl.ds(start, N_XY), :] = hits(owner_row == owner)
-        return unused
-
-    lax.fori_loop(0, CHUNKS, mark_owner, 0)
+    row256 = iota((SLOTS, SLOTS), 0).astype(F32).astype(BF16)
+    row128 = iota((CZ, SLOTS), 0).astype(F32)
+    row128_16 = row128.astype(BF16)
+    row32 = iota((N_XY, SLOTS), 0).astype(F32)
+
+    for c in range(CHUNKS):
+        owner_hits[c * N_XY : (c + 1) * N_XY, :] = hits(owner_row == (targets_ref[c] >> 12))
     before = hits(iota((SLOTS, SLOTS), 0) < iota((SLOTS, SLOTS), 1))
-    ones = jnp.ones((SLOTS, SLOTS), BF16)
-    rank_row = iota((SLOTS, SLOTS), 0)
-
-    def fill_slots(c, carry):
+    ranks_ref[...] = dot(owner_hits[...], before)
+    totals_ref[...] = dot(owner_hits[...], jnp.ones((SLOTS, SLOTS), BF16))
+
+    def fill_slots(g, carry):
         base, table = carry
-        start = pl.multiple_of(c * N_XY, N_XY)
-        marks = owner_hits[pl.ds(start, N_XY), :]
-        ranks = dot(marks, before) + base
-        base = base + dot(marks, ones)
-        target = targets_ref[c]
-        cell = cells_ref[c]
-        mine = owner_row == (target >> 12)
-        rank = jnp.sum(jnp.where(mine, ranks, 0.0), axis=0, keepdims=True).astype(jnp.int32)
-        place = target & 4095
-        fields = [
-            cell >> 7,
-            (cell & 127) + 1,
-            ((place >> 7) & 1) * 16 + (place >> 8),
-            place & 127,
-        ]
-        left = jnp.concatenate(
-            [jnp.where(mine, field.astype(F32), 0.0) for field in fields], axis=0
-        ).astype(BF16)
-        return base, table + dot_nt(left, hits(rank_row == rank))
+        lefts, rights = [], []
+        for k in range(GROUP):
+            c = g * GROUP + k
+            start = pl.multiple_of(c * N_XY, N_XY)
+            ranks = ranks_ref[pl.ds(start, N_XY), :] + base
+            base = base + totals_ref[pl.ds(start, N_XY), :]
+            target = targets_ref[c]
+            cell = cells_ref[c]
+            mine = owner_row == (target >> 12)
+            rank = jnp.sum(jnp.where(mine, ranks, 0.0), axis=0, keepdims=True)
+            place = target & 4095
+            fields = [
+                cell >> 7,
+                (cell & 127) + 1,
+                ((place >> 7) & 1) * 16 + (place >> 8),
+                place & 127,
+            ]
+            lefts.append(
+                jnp.concatenate(
+                    [jnp.where(mine, field.astype(F32), 0.0) for field in fields], axis=0
+                ).astype(BF16)
+            )
+            rights.append(hits16(row256, rank))
+        table = table + dot_nt(jnp.concatenate(lefts, axis=1), jnp.concatenate(rights, axis=1))
+        return base, table
 
     unused, table = lax.fori_loop(
         0,
-        CHUNKS,
+        CHUNKS // GROUP,
         fill_slots,
         (jnp.zeros((N_XY, SLOTS), F32), jnp.zeros((4 * N_XY, SLOTS), F32)),
     )
@@ -401,7 +445,15 @@
         slot_z[owner] = table[32 + owner : 33 + owner] - 1.0
         place_send[owner] = places[owner : owner + 1]
     place_recv[me] = place_send[me]
-    to_all(lambda other: place_send.at[other], place_recv, 1)
+    send_steps(lambda other: place_send.at[other], place_recv, 1, 0, OTHERS)
+
+    def mark_cells(g, unused):
+        for k in range(GROUP):
+            owner = g * GROUP + k
+            xy_hits[owner] = hits16(row256, slot_xy[owner])
+        return unused
+
+    lax.fori_loop(0, GROUPS, mark_cells, 0)
 
     for copy in halos:
         copy.wait_recv()
@@ -420,43 +472,38 @@
                     [roll(got, edge - (k * 4 + block), 1) for block in range(4)], axis=0
                 )
                 value = jnp.where(lane == edge, border, value)
-                rd[q, x + 1] = value
+            read_ref[q, x] = value
             term = WEIGHTS[q] * value
             total = term if total is None else total + term
         dens[pl.ds(pl.multiple_of(x * NY, NY), NY), :] = total
         return unused
 
     lax.fori_loop(0, CX, finish_plane, 0)
-    store = pltpu.make_async_copy(rd.at[:, pl.ds(1, CX)], read_hbm, store_sem)
-    store.start()
 
     high, low = split(jnp.transpose(dens[...]))
     dens_t = jnp.concatenate([high, low], axis=0)
-    row256 = iota((SLOTS, SLOTS), 0).astype(F32)
-    row128 = iota((CZ, SLOTS), 0).astype(F32)
-    row32 = iota((N_XY, SLOTS), 0).astype(F32)
-
-    def slot_density(owner):
-        found = dot(dens_t, hits(row256 == slot_xy[owner]))
-        both = found[0:128] + found[128:256]
-        return jnp.sum(jnp.where(row128 == slot_z[owner], both, 0.0), axis=0, keepdims=True)
-
-    def send_value(i, unused):
-        other = lax.rem(me + i, N_XY)
-        value_send[other] = slot_density(other)
-        pltpu.make_async_remote_copy(
-            src_ref=value_send.at[other],
-            dst_ref=value_recv.at[me],
-            send_sem=all_send.at[2],
-            recv_sem=all_recv.at[2],
-            device_id=(gz, other),
-            device_id_type=MESH,
-        ).start()
-        return unused
-
-    lax.fori_loop(1, N_XY, send_value, 0)
-    value_recv[me] = slot_density(me)
-    links = links_ref[...]
+
+    def send_values(g, unused):
+        others = [partner(me, g * GROUP + k) for k in range(GROUP)]
+        for other in others:
+            found = dot(dens_t, xy_hits[other])
+            both = found[0:128] + found[128:256]
+            value_send[other] = jnp.sum(
+                jnp.where(row128 == slot_z[other], both, 0.0), axis=0, keepdims=True
+            )
+        send_steps(
+            lambda other: value_send.at[other],
+            value_recv,
+            2,
+            g * GROUP,
+            jnp.minimum(g * GROUP + GROUP, OTHERS),
+        )
+        return unused
+
+    lax.fori_loop(0, GROUPS, send_values, 0)
+    value_recv[me] = value_send[me]
+
+    links = jnp.transpose(links_ref[...].astype(F32)).astype(jnp.int32)
     link_hits = []
     link_half = []
     lane256 = iota((16, 256), 1)
@@ -469,20 +516,35 @@
     all_copy(edge_recv0, 0).wait_recv()
     borders = gather_edges(edge_recv0[...].reshape(256, 128), link_hits, link_half)
     all_copy(place_recv, 1).wait_recv()
+
+    def mark_places(g, unused):
+        for k in range(GROUP):
+            brick = g * GROUP + k
+            place = place_recv[brick]
+            row = jnp.floor(place * (1.0 / 128.0))
+            place_row[brick] = row
+            lane_hits[brick] = hits16(row128_16, place - 128.0 * row)
+        return unused
+
+    lax.fori_loop(0, GROUPS, mark_places, 0)
     all_copy(value_recv, 2).wait_recv()
 
-    def add_supply(i, total):
-        value = value_recv[i]
-        place = place_recv[i]
-        row = jnp.floor(place * (1.0 / 128.0))
-        here = row32 == row
-        high = value.astype(BF16).astype(F32)
-        left = jnp.concatenate(
-            [jnp.where(here, high, 0.0), jnp.where(here, value - high, 0.0)], axis=0
-        ).astype(BF16)
-        return total + dot_nt(left, hits(row128 == place - 128.0 * row))
-
-    supply = lax.fori_loop(0, N_XY, add_supply, jnp.zeros((64, 128), F32))
+    def add_supply(g, total):
+        lefts, rights = [], []
+        for k in range(GROUP):
+            brick = g * GROUP + k
+            value = value_recv[brick]
+            here = row32 == place_row[brick]
+            high = value.astype(BF16).astype(F32)
+            lefts.append(
+                jnp.concatenate(
+                    [jnp.where(here, high, 0.0), jnp.where(here, value - high, 0.0)], axis=0
+                ).astype(BF16)
+            )
+            rights.append(lane_hits[brick])
+        return total + dot_nt(jnp.concatenate(lefts, axis=1), jnp.concatenate(rights, axis=1))
+
+    supply = lax.fori_loop(0, GROUPS, add_supply, jnp.zeros((64, 128), F32))
     supply = supply[0:32] + supply[32:64]
     supply = jnp.concatenate([supply[0:16], supply[16:32]], axis=1)
     source = cover + 0.3 * supply * (1.0 - cover) - 0.2 * cover
@@ -490,7 +552,7 @@
     edges = tile_edges(first, picker)
     edge_send1[...] = edges
     edge_recv1[me] = edges
-    to_all(lambda other: edge_send1, edge_recv1, 3)
+    send_steps(lambda other: edge_send1, edge_recv1, 3, 0, OTHERS)
     all_copy(edge_recv1, 3).wait_recv()
     borders = gather_edges(edge_recv1[...].reshape(256, 128), link_hits, link_half)
     second = sweep(first, source, borders, matrix)
@@ -500,46 +562,48 @@
     high, low = split(change)
     change = jnp.concatenate([high, low], axis=0)
 
-    def slot_change(brick):
-        place = place_recv[brick]
-        row = jnp.floor(place * (1.0 / 128.0))
-        found = dot(change, hits(row128 == place - 128.0 * row))
-        both = found[0:32] + found[32:64]
-        return jnp.sum(jnp.where(row32 == row, both, 0.0), axis=0, keepdims=True)
-
-    def send_change(i, unused):
-        other = lax.rem(me + i, N_XY)
-        change_send[other] = slot_change(other)
-        pltpu.make_async_remote_copy(
-            src_ref=change_send.at[other],
-            dst_ref=change_recv.at[me],
-            send_sem=all_send.at[4],
-            recv_sem=all_recv.at[4],
-            device_id=(gz, other),
-            device_id_type=MESH,
-        ).start()
-        return unused
-
-    lax.fori_loop(1, N_XY, send_change, 0)
-    change_recv[me] = slot_change(me)
+    def send_changes(g, unused):
+        others = [partner(me, g * GROUP + k) for k in range(GROUP)]
+        for other in others:
+            found = dot(change, lane_hits[other])
+            both = found[0:32] + found[32:64]
+            change_send[other] = jnp.sum(
+                jnp.where(row32 == place_row[other], both, 0.0), axis=0, keepdims=True
+            )
+        send_steps(
+            lambda other: change_send.at[other],
+            change_recv,
+            4,
+            g * GROUP,
+            jnp.minimum(g * GROUP + GROUP, OTHERS),
+        )
+        return unused
+
+    lax.fori_loop(0, GROUPS, send_changes, 0)
+    change_recv[me] = change_send[me]
     corr_acc[...] = jnp.zeros_like(corr_acc)
-    all_copy(change_recv, 4).wait_recv()
-
-    def add_change(owner, unused):
-        value = change_recv[owner]
-        here = row128 == slot_z[owner]
-        high = value.astype(BF16).astype(F32)
-        right = jnp.concatenate(
-            [jnp.where(here, high, 0.0), jnp.where(here, value - high, 0.0)], axis=0
-        ).astype(BF16)
-        corr_acc[...] += dot_nt(hits(row256 == slot_xy[owner]), right)
-        return unused
-
-    lax.fori_loop(0, N_XY, add_change, 0)
-    correction_out[...] = corr_acc[:, 0:128] + corr_acc[:, 128:256]
-
     for copy in halos:
         copy.wait_send()
+    all_copy(change_recv, 4).wait_recv()
+
+    def add_change(g, unused):
+        lefts, rights = [], []
+        for k in range(GROUP):
+            owner = g * GROUP + k
+            value = change_recv[owner]
+            here = row128 == slot_z[owner]
+            high = value.astype(BF16).astype(F32)
+            rights.append(
+                jnp.concatenate(
+                    [jnp.where(here, high, 0.0), jnp.where(here, value - high, 0.0)], axis=0
+                ).astype(BF16)
+            )
+            lefts.append(xy_hits[owner])
+        corr_acc[...] += dot_nt(jnp.concatenate(lefts, axis=1), jnp.concatenate(rights, axis=1))
+        return unused
+
+    lax.fori_loop(0, GROUPS, add_change, 0)
+    correction_out[...] = corr_acc[:, 0:128] + corr_acc[:, 128:256]
     for ref, index in (
         (edge_recv0, 0),
         (place_recv, 1),
@@ -548,27 +612,42 @@
         (change_recv, 4),
     ):
         all_copy(ref, index).wait_send()
-    store.wait()
+
+
+def add_kernel(read_ref, correction_ref, cover_ref, updated_hbm, cover_hbm, stage, sem):
+    cover_copy = pltpu.make_async_copy(cover_ref, cover_hbm, sem.at[CX])
+    cover_copy.start()
+    copies = []
+    for x in range(CX):
+        stage[:, x] = read_ref[:, x] + correction_ref[x * NY : (x + 1) * NY, :][None]
+        copies.append(pltpu.make_async_copy(stage.at[:, x], updated_hbm.at[:, x], sem.at[x]))
+        copies[-1].start()
+    for copy in copies:
+        copy.wait()
+    cover_copy.wait()
 
 
 def shards(populations, solid, knudsen, wall_cells, wall_target, coverage, tile_links):
-    anywhere = pl.BlockSpec(memory_space=pl.ANY)
+    hbm = pl.BlockSpec(memory_space=pltpu.HBM)
     vmem = pl.BlockSpec(memory_space=pltpu.VMEM)
     slots = pltpu.VMEM((N_XY, 1, SLOTS), F32)
     edge_table = pltpu.VMEM((N_XY, 8, 128), F32)
+    walls = pltpu.VMEM((CHUNKS, 1, SLOTS), jnp.int32)
+    whole = jax.ShapeDtypeStruct((19, CX, NY, CZ), F32)
+    cover_shape = jax.ShapeDtypeStruct((16, 256), F32)
     read, new_coverage, correction = pl.pallas_call(
         kernel,
-        out_shape=(
-            jax.ShapeDtypeStruct((19, CX, NY, CZ), F32),
-            jax.ShapeDtypeStruct((16, 256), F32),
-            jax.ShapeDtypeStruct((256, 128), F32),
-        ),
-        in_specs=[anywhere] * 3 + [vmem] * 4,
-        out_specs=(anywhere, vmem, vmem),
+        out_shape=(whole, cover_shape, jax.ShapeDtypeStruct((256, 128), F32)),
+        in_specs=[hbm] * 7,
+        out_specs=(vmem, vmem, vmem),
         scratch_shapes=[
             pltpu.VMEM((19, CX, NY, CZ), F32),
             pltpu.VMEM((CX, NY, CZ), jnp.int32),
             pltpu.VMEM((CX, NY, CZ), F32),
+            walls,
+            walls,
+            pltpu.VMEM((16, 256), F32),
+            pltpu.VMEM((4, 16), jnp.int32),
             pltpu.VMEM((19, CX + 2, NY, CZ), F32),
             pltpu.VMEM((CX, 8, 128), F32),
             pltpu.VMEM((CX, 8, 128), F32),
@@ -576,6 +655,11 @@
             pltpu.VMEM((CX + 2, 8, 128), F32),
             pltpu.VMEM((CX * NY, CZ), F32),
             pltpu.VMEM((CHUNKS * N_XY, SLOTS), BF16),
+            pltpu.VMEM((CHUNKS * N_XY, SLOTS), F32),
+            pltpu.VMEM((CHUNKS * N_XY, SLOTS), F32),
+            pltpu.VMEM((N_XY, SLOTS, SLOTS), BF16),
+            pltpu.VMEM((N_XY, CZ, SLOTS), BF16),
+            slots,
             slots,
             slots,
             slots,
@@ -589,26 +673,40 @@
             pltpu.VMEM((8, 128), F32),
             edge_table,
             pltpu.VMEM((256, 256), F32),
-            pltpu.SemaphoreType.DMA((10,)),
-            pltpu.SemaphoreType.DMA,
+            pltpu.SemaphoreType.DMA((14,)),
             pltpu.SemaphoreType.DMA((16,)),
             pltpu.SemaphoreType.DMA((16,)),
             pltpu.SemaphoreType.DMA((5,)),
             pltpu.SemaphoreType.DMA((5,)),
         ],
         compiler_params=pltpu.CompilerParams(
-            collective_id=0, has_side_effects=True, vmem_limit_bytes=32 * 1024 * 1024
+            collective_id=0, has_side_effects=True, vmem_limit_bytes=40 * 1024 * 1024
         ),
     )(
-        populations,
-        solid,
-        knudsen,
-        wall_cells.reshape(CHUNKS, 1, SLOTS),
-        wall_target.reshape(CHUNKS, 1, SLOTS),
-        coverage,
-        tile_links,
+        *[
+            pltpu.with_memory_space_constraint(array, pltpu.HBM)
+            for array in (
+                populations,
+                solid,
+                knudsen,
+                wall_cells.reshape(CHUNKS, 1, SLOTS),
+                wall_target.reshape(CHUNKS, 1, SLOTS),
+                coverage,
+                tile_links.T,
+            )
+        ]
     )
-    updated = read + correction.reshape(1, CX, NY, CZ)
+    updated, new_coverage = pl.pallas_call(
+        add_kernel,
+        out_shape=(whole, cover_shape),
+        in_specs=[vmem, vmem, vmem],
+        out_specs=(hbm, hbm),
+        scratch_shapes=[
+            pltpu.VMEM((19, CX, NY, CZ), F32),
+            pltpu.SemaphoreType.DMA((CX + 1,)),
+        ],
+        compiler_params=pltpu.CompilerParams(vmem_limit_bytes=16 * 1024 * 1024),
+    )(read, correction, new_coverage)
     return updated, new_coverage
 
 

time: 69.5 us -> 47 us (0.68)
  Pallas kernels: 59.7 us -> 46 us
  local copies, waits for them, and re-layouts: 7.02 us -> 0 us
  other arithmetic: 1.74 us -> 0 us
    pallas_call x1 -> x2, Pallas kernels: 59.7 us -> 46 us  [the longest x1 44.5 us: shards(): pl.pallas_call(kernel, out_shape=(whole, cover_shape, jax.ShapeDtypeStruc...]
    unnamed x14 -> x0, local copies, waits for them, and re-layouts: 7.02 us -> none
    add x1 -> x0, other arithmetic: 1.74 us -> none  [shards(): updated = read + correction.reshape(1, CX, NY, CZ)]
where the time goes in v2:
time: 47 us; the launch traced here: 46.7 us
  Pallas kernels  46 us (98%)
  between operations  0.64 us (1%)
    pallas_call x1, Pallas kernels, shards(): pl.pallas_call(kernel, out_shape=(whole, cover_shape, jax.ShapeDtypeStruc...  44.5 us
    pallas_call x1, Pallas kernels, shards(): pl.pallas_call(add_kernel, out_shape=(whole, cover_shape), in_specs=[vmem...  1.54 us

profile of v2, /device:TPU:8, one launch (start us, length us, event | category | flops | bytes accessed | tf_op | source)
XLA Modules:
  0.0 46.7 jit_solution(13077688666281575439)
XLA Ops:
  0.6 44.5 %shard_map.86 = (f32[19,8,32,128]{3,2,1,0:T(8,128)S(1)}, f32[16,256]{1,0:T(8,128)S(1)}, f32[256,128]{1,0:T(8,128)S(1)}) custom-call(f32[19,8,32,128]{3,2,1,0:T(8,128)} %pop_hbm.1, s32[8,32,128]{2,1,0:T(8,128)} %solid_hbm.1, f32[8,32,128]{2,1,0:T(8,128)} %knudsen_hbm.1, s32[16,1,256]{2,1,0:T(1,128)} %bitcast.3, s32[16,1,256]{2,1,0:T(1,128)} %bitcast.4, ...), custom_call_target="tpu_custom_call" | custom-call | tf_op jit(solution)/shard_map/pallas_call | solution.py:638
  45.1 1.5 %shard_map.87 = (f32[19,8,32,128]{3,2,1,0:T(8,128)}, f32[16,256]{1,0:T(8,128)}) custom-call(f32[19,8,32,128]{3,2,1,0:T(8,128)S(1)} %get-tuple-element.5.read_ref, f32[256,128]{1,0:T(8,128)S(1)} %get-tuple-element.6.correction_ref, f32[16,256]{1,0:T(8,128)S(1)} %get-tuple-element.7.cover_ref), custom_call_target="tpu_custom_call" | custom-call | tf_op jit(solution)/shard_map/pallas_call | solution.py:699

commit v3 on v2

--- a/solution.py
+++ b/solution.py
@@ -45,7 +45,7 @@
 CHUNKS = 16
 OTHERS = N_XY - 1
 GREETED = OTHERS + 6
-GROUP = 4
+GROUP = 8
 GROUPS = N_XY // GROUP
 
 
@@ -187,7 +187,16 @@
     edge_recv0,
     edge_send1,
     edge_recv1,
-    corr_acc,
+    link_send,
+    link_recv,
+    link_table,
+    cell_hits,
+    rank_hits,
+    across_hits,
+    along_hits,
+    across_place,
+    along_place,
+    border_terms,
     load_sem,
     halo_send,
     halo_recv,
@@ -198,6 +207,25 @@
     me = lax.axis_index("xy")
     gz_up, gz_down = lax.rem(gz + 1, N_GZ), lax.rem(gz + N_GZ - 1, N_GZ)
     up, down = lax.rem(me + 1, N_XY), lax.rem(me + N_XY - 1, N_XY)
+
+    barrier = pltpu.get_barrier_semaphore()
+
+    def greet(i, unused):
+        pl.semaphore_signal(
+            barrier, inc=1, device_id=(gz, partner(me, i)), device_id_type=MESH
+        )
+        return unused
+
+    lax.fori_loop(0, OTHERS, greet, 0)
+    for device in (
+        (gz_up, up),
+        (gz_up, down),
+        (gz_down, up),
+        (gz_down, down),
+        (gz_up, me),
+        (gz_down, me),
+    ):
+        pl.semaphore_signal(barrier, inc=1, device_id=device, device_id_type=MESH)
 
     def load(source, target, index):
         copy = pltpu.make_async_copy(source, target, load_sem.at[index])
@@ -216,25 +244,6 @@
         load(cover_hbm, cover_ref, 12),
         load(links_hbm, links_ref, 13),
     ]
-
-    barrier = pltpu.get_barrier_semaphore()
-
-    def greet(i, unused):
-        pl.semaphore_signal(
-            barrier, inc=1, device_id=(gz, partner(me, i)), device_id_type=MESH
-        )
-        return unused
-
-    lax.fori_loop(0, OTHERS, greet, 0)
-    for device in (
-        (gz_up, up),
-        (gz_up, down),
-        (gz_down, up),
-        (gz_down, down),
-        (gz_up, me),
-        (gz_down, me),
-    ):
-        pl.semaphore_signal(barrier, inc=1, device_id=device, device_id_type=MESH)
 
     def send_one(source, target, index, other):
         pltpu.make_async_remote_copy(
@@ -362,36 +371,11 @@
     for copy in cell_loads + [plane_loads[0], plane_loads[7]]:
         copy.wait()
     lax.fori_loop(0, 2, edge_step, 0)
-    pl.semaphore_wait(barrier, GREETED)
-    halos = []
-    halos.append(halo(zs_p.at[7], zr_p.at[0], 12, (gz_up, up)))
-    halos.append(halo(zs_p.at[0], zr_p.at[9], 13, (gz_up, down)))
-    halos.append(halo(zs_m.at[7], zr_m.at[0], 14, (gz_down, up)))
-    halos.append(halo(zs_m.at[0], zr_m.at[9], 15, (gz_down, down)))
-    for k in range(5):
-        halos.append(halo(rd.at[X_PLUS[k], 9], rd.at[X_PLUS[k], 1], k, (gz, up)))
-        halos.append(halo(rd.at[X_MINUS[k], 0], rd.at[X_MINUS[k], 8], 5 + k, (gz, down)))
-    for copy in halos:
-        copy.start()
     for x in range(1, 7):
         plane_loads[x].wait()
     lax.fori_loop(1, 7, inner_step, 0)
-    faces = [
-        halo(zs_p, zr_p.at[pl.ds(1, CX)], 10, (gz_up, me)),
-        halo(zs_m, zr_m.at[pl.ds(1, CX)], 11, (gz_down, me)),
-    ]
-    for copy in faces:
-        copy.start()
-    halos = halos + faces
     for copy in wall_loads:
         copy.wait()
-
-    picker = edge_picker()
-    cover = cover_ref[...]
-    edges = tile_edges(cover, picker)
-    edge_send0[...] = edges
-    edge_recv0[me] = edges
-    send_steps(lambda other: edge_send0, edge_recv0, 0, 0, OTHERS)
 
     owner_row = iota((N_XY, SLOTS), 0)
     row256 = iota((SLOTS, SLOTS), 0).astype(F32).astype(BF16)
@@ -429,7 +413,9 @@
                     [jnp.where(mine, field.astype(F32), 0.0) for field in fields], axis=0
                 ).astype(BF16)
             )
-            rights.append(hits16(row256, rank))
+            rank_hits[c] = hits16(row256, rank)
+            cell_hits[c] = hits16(row256, fields[0].astype(F32))
+            rights.append(rank_hits[c])
         table = table + dot_nt(jnp.concatenate(lefts, axis=1), jnp.concatenate(rights, axis=1))
         return base, table
 
@@ -445,7 +431,33 @@
         slot_z[owner] = table[32 + owner : 33 + owner] - 1.0
         place_send[owner] = places[owner : owner + 1]
     place_recv[me] = place_send[me]
+
+    picker = edge_picker()
+    cover = cover_ref[...]
+    edges = tile_edges(cover, picker)
+    edge_send0[...] = edges
+    edge_recv0[me] = edges
+    links = links_ref[...]
+    codes = (links >> 4) * 8 + (links & 7) + ((links >> 3) & 1) * 256
+    link_send[...] = jnp.zeros_like(link_send)
+    link_send[:, 0:16] = codes.astype(F32)
+    link_recv[me] = link_send[...]
+    pl.semaphore_wait(barrier, GREETED)
+    halos = []
+    halos.append(halo(zs_p.at[7], zr_p.at[0], 12, (gz_up, up)))
+    halos.append(halo(zs_p.at[0], zr_p.at[9], 13, (gz_up, down)))
+    halos.append(halo(zs_m.at[7], zr_m.at[0], 14, (gz_down, up)))
+    halos.append(halo(zs_m.at[0], zr_m.at[9], 15, (gz_down, down)))
+    for k in range(5):
+        halos.append(halo(rd.at[X_PLUS[k], 9], rd.at[X_PLUS[k], 1], k, (gz, up)))
+        halos.append(halo(rd.at[X_MINUS[k], 0], rd.at[X_MINUS[k], 8], 5 + k, (gz, down)))
+    halos.append(halo(zs_p, zr_p.at[pl.ds(1, CX)], 10, (gz_up, me)))
+    halos.append(halo(zs_m, zr_m.at[pl.ds(1, CX)], 11, (gz_down, me)))
+    for copy in halos:
+        copy.start()
     send_steps(lambda other: place_send.at[other], place_recv, 1, 0, OTHERS)
+    send_steps(lambda other: link_send, link_recv, 5, 0, OTHERS)
+    send_steps(lambda other: edge_send0, edge_recv0, 0, 0, OTHERS)
 
     def mark_cells(g, unused):
         for k in range(GROUP):
@@ -527,6 +539,38 @@
         return unused
 
     lax.fori_loop(0, GROUPS, mark_places, 0)
+    all_copy(link_recv, 5).wait_recv()
+    for owner in range(N_XY):
+        link_table[owner * 4 : owner * 4 + 4, :] = link_recv[owner]
+    codes = jnp.transpose(link_table[...])[0:16]
+    second_half = jnp.where(codes >= 256.0, 1.0, 0.0)
+    codes = jnp.concatenate([codes - 256.0 * second_half, second_half], axis=0).astype(BF16)
+    row16 = iota((16, SLOTS), 0)
+
+    def find_border(select, tile, valid, far, place):
+        found = dot(codes, hits16(row128_16, select.astype(F32)))
+        here = row16 == tile
+        row = jnp.sum(jnp.where(here, found[0:16], 0.0), axis=0, keepdims=True)
+        half = jnp.sum(jnp.where(here, found[16:32], 0.0), axis=0, keepdims=True)
+        return jnp.where(valid, row, -1.0), half * 32.0 + (far * 16 + place).astype(F32)
+
+    def mark_borders(g, unused):
+        for k in range(GROUP):
+            c = g * GROUP + k
+            target = targets_ref[c]
+            owner, tile = target >> 12, (target >> 8) & 15
+            y, x = (target >> 4) & 15, target & 15
+            far_x = jnp.where(x == 15, 1, 0)
+            far_y = jnp.where(y == 15, 1, 0)
+            row, place = find_border(owner * 4 + far_x, tile, (x == 0) | (x == 15), far_x, y)
+            across_hits[c] = hits16(row256, row)
+            across_place[c] = place
+            row, place = find_border(owner * 4 + 2 + far_y, tile, (y == 0) | (y == 15), far_y, x)
+            along_hits[c] = hits16(row256, row)
+            along_place[c] = place
+        return unused
+
+    lax.fori_loop(0, CHUNKS // GROUP, mark_borders, 0)
     all_copy(value_recv, 2).wait_recv()
 
     def add_supply(g, total):
@@ -553,10 +597,9 @@
     edge_send1[...] = edges
     edge_recv1[me] = edges
     send_steps(lambda other: edge_send1, edge_recv1, 3, 0, OTHERS)
-    all_copy(edge_recv1, 3).wait_recv()
-    borders = gather_edges(edge_recv1[...].reshape(256, 128), link_hits, link_half)
-    second = sweep(first, source, borders, matrix)
-    cover_out[...] = second
+    high, low = split(first)
+    second = dot(jnp.concatenate([high, low], axis=1), matrix[0:512])
+    second = (source + 2.0 * second) * (1.0 / 9.0)
     change = -0.5 * (second - cover)
     change = jnp.concatenate([change[:, 0:128], change[:, 128:256]], axis=0)
     high, low = split(change)
@@ -581,35 +624,66 @@
 
     lax.fori_loop(0, GROUPS, send_changes, 0)
     change_recv[me] = change_send[me]
-    corr_acc[...] = jnp.zeros_like(corr_acc)
     for copy in halos:
         copy.wait_send()
+    all_copy(edge_recv1, 3).wait_recv()
+    table = edge_recv1[...].reshape(256, 128)
+    borders = gather_edges(table, link_hits, link_half)
+    cover_out[...] = second + dot(borders.astype(BF16), matrix[512:640]) * (2.0 / 9.0)
+    table = jnp.transpose(table)
+    high, low = split(jnp.concatenate([table[0:32], table[64:96]], axis=0))
+    across = jnp.concatenate([high, low], axis=0)
+    high, low = split(jnp.concatenate([table[32:64], table[96:128]], axis=0))
+    along = jnp.concatenate([high, low], axis=0)
+    row64 = iota((64, SLOTS), 0).astype(F32)
+
+    def add_borders(g, unused):
+        for k in range(GROUP):
+            c = g * GROUP + k
+            found = dot(across, across_hits[c])
+            total = jnp.where(row64 == across_place[c], found[0:64] + found[64:128], 0.0)
+            found = dot(along, along_hits[c])
+            total = total + jnp.where(
+                row64 == along_place[c], found[0:64] + found[64:128], 0.0
+            )
+            border_terms[c] = jnp.sum(total, axis=0, keepdims=True) * (-1.0 / 9.0)
+        return unused
+
+    lax.fori_loop(0, CHUNKS // GROUP, add_borders, 0)
     all_copy(change_recv, 4).wait_recv()
-
-    def add_change(g, unused):
+    got = jnp.concatenate([change_recv[owner] for owner in range(N_XY)], axis=0)
+    high, low = split(got)
+    got = jnp.concatenate([high, low], axis=0)
+
+    def add_change(g, total):
         lefts, rights = [], []
         for k in range(GROUP):
-            owner = g * GROUP + k
-            value = change_recv[owner]
-            here = row128 == slot_z[owner]
+            c = g * GROUP + k
+            found = dot(got, rank_hits[c])
+            mine = owner_row == (targets_ref[c] >> 12)
+            value = jnp.sum(
+                jnp.where(mine, found[0:32] + found[32:64], 0.0), axis=0, keepdims=True
+            )
+            value = value + border_terms[c]
+            here = row128 == (cells_ref[c] & 127).astype(F32)
             high = value.astype(BF16).astype(F32)
             rights.append(
                 jnp.concatenate(
                     [jnp.where(here, high, 0.0), jnp.where(here, value - high, 0.0)], axis=0
                 ).astype(BF16)
             )
-            lefts.append(xy_hits[owner])
-        corr_acc[...] += dot_nt(jnp.concatenate(lefts, axis=1), jnp.concatenate(rights, axis=1))
-        return unused
-
-    lax.fori_loop(0, GROUPS, add_change, 0)
-    correction_out[...] = corr_acc[:, 0:128] + corr_acc[:, 128:256]
+            lefts.append(cell_hits[c])
+        return total + dot_nt(jnp.concatenate(lefts, axis=1), jnp.concatenate(rights, axis=1))
+
+    correction = lax.fori_loop(0, CHUNKS // GROUP, add_change, jnp.zeros((256, 256), F32))
+    correction_out[...] = correction[:, 0:128] + correction[:, 128:256]
     for ref, index in (
         (edge_recv0, 0),
         (place_recv, 1),
         (value_recv, 2),
         (edge_recv1, 3),
         (change_recv, 4),
+        (link_recv, 5),
     ):
         all_copy(ref, index).wait_send()
 
@@ -632,6 +706,8 @@
     vmem = pl.BlockSpec(memory_space=pltpu.VMEM)
     slots = pltpu.VMEM((N_XY, 1, SLOTS), F32)
     edge_table = pltpu.VMEM((N_XY, 8, 128), F32)
+    by_chunk = pltpu.VMEM((CHUNKS, SLOTS, SLOTS), BF16)
+    chunk_rows = pltpu.VMEM((CHUNKS, 1, SLOTS), F32)
     walls = pltpu.VMEM((CHUNKS, 1, SLOTS), jnp.int32)
     whole = jax.ShapeDtypeStruct((19, CX, NY, CZ), F32)
     cover_shape = jax.ShapeDtypeStruct((16, 256), F32)
@@ -672,12 +748,21 @@
             edge_table,
             pltpu.VMEM((8, 128), F32),
             edge_table,
-            pltpu.VMEM((256, 256), F32),
+            pltpu.VMEM((4, 128), F32),
+            pltpu.VMEM((N_XY, 4, 128), F32),
+            pltpu.VMEM((4 * N_XY, 128), F32),
+            by_chunk,
+            by_chunk,
+            by_chunk,
+            by_chunk,
+            chunk_rows,
+            chunk_rows,
+            chunk_rows,
             pltpu.SemaphoreType.DMA((14,)),
             pltpu.SemaphoreType.DMA((16,)),
             pltpu.SemaphoreType.DMA((16,)),
-            pltpu.SemaphoreType.DMA((5,)),
-            pltpu.SemaphoreType.DMA((5,)),
+            pltpu.SemaphoreType.DMA((6,)),
+            pltpu.SemaphoreType.DMA((6,)),
         ],
         compiler_params=pltpu.CompilerParams(
             collective_id=0, has_side_effects=True, vmem_limit_bytes=40 * 1024 * 1024

time: 47 us -> 40.4 us (0.86)
  Pallas kernels: 46 us -> 39.6 us
    pallas_call x1, Pallas kernels: 44.5 us -> 38.1 us  [shards(): pl.pallas_call(kernel, out_shape=(whole, cover_shape, jax.ShapeDtypeStruc...]
where the time goes in v3:
time: 40.4 us; the launch traced here: 40.3 us
  Pallas kernels  39.6 us (98%)
  between operations  0.64 us (2%)
    pallas_call x1, Pallas kernels, shards(): pl.pallas_call(kernel, out_shape=(whole, cover_shape, jax.ShapeDtypeStruc...  38.1 us
    pallas_call x1, Pallas kernels, shards(): pl.pallas_call(add_kernel, out_shape=(whole, cover_shape), in_specs=[vmem...  1.54 us

profile of v3, /device:TPU:8, one launch (start us, length us, event | category | flops | bytes accessed | tf_op | source)
XLA Modules:
  0.0 40.3 jit_solution(18084126732932161361)
XLA Ops:
  0.6 38.1 %shard_map.86 = (f32[19,8,32,128]{3,2,1,0:T(8,128)S(1)}, f32[16,256]{1,0:T(8,128)S(1)}, f32[256,128]{1,0:T(8,128)S(1)}) custom-call(f32[19,8,32,128]{3,2,1,0:T(8,128)} %pop_hbm.1, s32[8,32,128]{2,1,0:T(8,128)} %solid_hbm.1, f32[8,32,128]{2,1,0:T(8,128)} %knudsen_hbm.1, s32[16,1,256]{2,1,0:T(1,128)} %bitcast.3, s32[16,1,256]{2,1,0:T(1,128)} %bitcast.4, ...), custom_call_target="tpu_custom_call" | custom-call | tf_op jit(solution)/shard_map/pallas_call | solution.py:714
  38.7 1.5 %shard_map.87 = (f32[19,8,32,128]{3,2,1,0:T(8,128)}, f32[16,256]{1,0:T(8,128)}) custom-call(f32[19,8,32,128]{3,2,1,0:T(8,128)S(1)} %get-tuple-element.5.read_ref, f32[256,128]{1,0:T(8,128)S(1)} %get-tuple-element.6.correction_ref, f32[16,256]{1,0:T(8,128)S(1)} %get-tuple-element.7.cover_ref), custom_call_target="tpu_custom_call" | custom-call | tf_op jit(solution)/shard_map/pallas_call | solution.py:784

commit v4 on v3

--- a/solution.py
+++ b/solution.py
@@ -44,7 +44,8 @@
 SLOTS = 256
 CHUNKS = 16
 OTHERS = N_XY - 1
-GREETED = OTHERS + 6
+NEAR = 19
+GREETED = NEAR + 6
 GROUP = 8
 GROUPS = N_XY // GROUP
 
@@ -200,6 +201,7 @@
     load_sem,
     halo_send,
     halo_recv,
+    ready_sem,
     all_send,
     all_recv,
 ):
@@ -207,25 +209,6 @@
     me = lax.axis_index("xy")
     gz_up, gz_down = lax.rem(gz + 1, N_GZ), lax.rem(gz + N_GZ - 1, N_GZ)
     up, down = lax.rem(me + 1, N_XY), lax.rem(me + N_XY - 1, N_XY)
-
-    barrier = pltpu.get_barrier_semaphore()
-
-    def greet(i, unused):
-        pl.semaphore_signal(
-            barrier, inc=1, device_id=(gz, partner(me, i)), device_id_type=MESH
-        )
-        return unused
-
-    lax.fori_loop(0, OTHERS, greet, 0)
-    for device in (
-        (gz_up, up),
-        (gz_up, down),
-        (gz_down, up),
-        (gz_down, down),
-        (gz_up, me),
-        (gz_down, me),
-    ):
-        pl.semaphore_signal(barrier, inc=1, device_id=device, device_id_type=MESH)
 
     def load(source, target, index):
         copy = pltpu.make_async_copy(source, target, load_sem.at[index])
@@ -244,6 +227,34 @@
         load(cover_hbm, cover_ref, 12),
         load(links_hbm, links_ref, 13),
     ]
+
+    barrier = pltpu.get_barrier_semaphore()
+
+    def near(i):
+        step = jnp.where(i >= 8, i + 1, i)
+        z = (me % 8 + step // 4 + 6) % 8
+        x = (me // 8 + step % 4) % 4
+        return x * 8 + z
+
+    def greet_near(semaphore):
+        def greet(i, unused):
+            pl.semaphore_signal(
+                semaphore, inc=1, device_id=(gz, near(i)), device_id_type=MESH
+            )
+            return unused
+
+        lax.fori_loop(0, NEAR, greet, 0)
+
+    for device in (
+        (gz_up, up),
+        (gz_up, down),
+        (gz_down, up),
+        (gz_down, down),
+        (gz_up, me),
+        (gz_down, me),
+    ):
+        pl.semaphore_signal(barrier, inc=1, device_id=device, device_id_type=MESH)
+    greet_near(barrier)
 
     def send_one(source, target, index, other):
         pltpu.make_async_remote_copy(
@@ -371,9 +382,28 @@
     for copy in cell_loads + [plane_loads[0], plane_loads[7]]:
         copy.wait()
     lax.fori_loop(0, 2, edge_step, 0)
+    pl.semaphore_wait(barrier, GREETED)
+    halos = []
+    halos.append(halo(zs_p.at[7], zr_p.at[0], 12, (gz_up, up)))
+    halos.append(halo(zs_p.at[0], zr_p.at[9], 13, (gz_up, down)))
+    halos.append(halo(zs_m.at[7], zr_m.at[0], 14, (gz_down, up)))
+    halos.append(halo(zs_m.at[0], zr_m.at[9], 15, (gz_down, down)))
+    for k in range(5):
+        halos.append(halo(rd.at[X_PLUS[k], 9], rd.at[X_PLUS[k], 1], k, (gz, up)))
+        halos.append(halo(rd.at[X_MINUS[k], 0], rd.at[X_MINUS[k], 8], 5 + k, (gz, down)))
+    for copy in halos:
+        copy.start()
+    greet_near(ready_sem)
     for x in range(1, 7):
         plane_loads[x].wait()
     lax.fori_loop(1, 7, inner_step, 0)
+    faces = [
+        halo(zs_p, zr_p.at[pl.ds(1, CX)], 10, (gz_up, me)),
+        halo(zs_m, zr_m.at[pl.ds(1, CX)], 11, (gz_down, me)),
+    ]
+    for copy in faces:
+        copy.start()
+    halos = halos + faces
     for copy in wall_loads:
         copy.wait()
 
@@ -442,22 +472,6 @@
     link_send[...] = jnp.zeros_like(link_send)
     link_send[:, 0:16] = codes.astype(F32)
     link_recv[me] = link_send[...]
-    pl.semaphore_wait(barrier, GREETED)
-    halos = []
-    halos.append(halo(zs_p.at[7], zr_p.at[0], 12, (gz_up, up)))
-    halos.append(halo(zs_p.at[0], zr_p.at[9], 13, (gz_up, down)))
-    halos.append(halo(zs_m.at[7], zr_m.at[0], 14, (gz_down, up)))
-    halos.append(halo(zs_m.at[0], zr_m.at[9], 15, (gz_down, down)))
-    for k in range(5):
-        halos.append(halo(rd.at[X_PLUS[k], 9], rd.at[X_PLUS[k], 1], k, (gz, up)))
-        halos.append(halo(rd.at[X_MINUS[k], 0], rd.at[X_MINUS[k], 8], 5 + k, (gz, down)))
-    halos.append(halo(zs_p, zr_p.at[pl.ds(1, CX)], 10, (gz_up, me)))
-    halos.append(halo(zs_m, zr_m.at[pl.ds(1, CX)], 11, (gz_down, me)))
-    for copy in halos:
-        copy.start()
-    send_steps(lambda other: place_send.at[other], place_recv, 1, 0, OTHERS)
-    send_steps(lambda other: link_send, link_recv, 5, 0, OTHERS)
-    send_steps(lambda other: edge_send0, edge_recv0, 0, 0, OTHERS)
 
     def mark_cells(g, unused):
         for k in range(GROUP):
@@ -467,30 +481,63 @@
 
     lax.fori_loop(0, GROUPS, mark_cells, 0)
 
+    def border(q, x):
+        cx, cy, cz = VELOCITIES[q]
+        k = (Z_PLUS if cz == 1 else Z_MINUS).index(q)
+        got = (zr_p if cz == 1 else zr_m)[x - cx + 1]
+        edge = 0 if cz == 1 else 127
+        return jnp.concatenate(
+            [roll(got, edge - (k * 4 + block), 1) for block in range(4)], axis=0
+        )
+
+    def inner_plane(x, unused):
+        total = None
+        for q in range(19):
+            value = rd[q, x + 1]
+            read_ref[q, x] = value
+            term = WEIGHTS[q] * value
+            total = term if total is None else total + term
+        dens[pl.ds(pl.multiple_of(x * NY, NY), NY), :] = total
+        return unused
+
+    lax.fori_loop(1, CX - 1, inner_plane, 0)
+    pl.semaphore_wait(ready_sem, NEAR)
+    send_steps(lambda other: place_send.at[other], place_recv, 1, 0, OTHERS)
+    send_steps(lambda other: edge_send0, edge_recv0, 0, 0, OTHERS)
+
     for copy in halos:
         copy.wait_recv()
 
-    def finish_plane(x, unused):
+    def finish_plane(i, unused):
+        x = i * 7
         lane = iota((NY, CZ), 1)
         total = None
         for q in range(19):
             cx, cy, cz = VELOCITIES[q]
             value = rd[q, x + 1]
             if cz != 0:
-                k = (Z_PLUS if cz == 1 else Z_MINUS).index(q)
-                got = (zr_p if cz == 1 else zr_m)[x - cx + 1]
-                edge = 0 if cz == 1 else 127
-                border = jnp.concatenate(
-                    [roll(got, edge - (k * 4 + block), 1) for block in range(4)], axis=0
-                )
-                value = jnp.where(lane == edge, border, value)
+                value = jnp.where(lane == (0 if cz == 1 else 127), border(q, x), value)
             read_ref[q, x] = value
             term = WEIGHTS[q] * value
             total = term if total is None else total + term
         dens[pl.ds(pl.multiple_of(x * NY, NY), NY), :] = total
         return unused
 
-    lax.fori_loop(0, CX, finish_plane, 0)
+    def mend_plane(x, unused):
+        lane = iota((NY, CZ), 1)
+        rows = pl.ds(pl.multiple_of(x * NY, NY), NY)
+        total = dens[rows, :]
+        for members, edge in ((Z_PLUS, 0), (Z_MINUS, 127)):
+            for q in members:
+                old = read_ref[q, x]
+                new = jnp.where(lane == edge, border(q, x), old)
+                read_ref[q, x] = new
+                total = total + WEIGHTS[q] * (new - old)
+        dens[rows, :] = total
+        return unused
+
+    lax.fori_loop(1, CX - 1, mend_plane, 0)
+    lax.fori_loop(0, 2, finish_plane, 0)
 
     high, low = split(jnp.transpose(dens[...]))
     dens_t = jnp.concatenate([high, low], axis=0)
@@ -514,6 +561,7 @@
 
     lax.fori_loop(0, GROUPS, send_values, 0)
     value_recv[me] = value_send[me]
+    send_steps(lambda other: link_send, link_recv, 5, 0, OTHERS)
 
     links = jnp.transpose(links_ref[...].astype(F32)).astype(jnp.int32)
     link_hits = []
@@ -539,38 +587,6 @@
         return unused
 
     lax.fori_loop(0, GROUPS, mark_places, 0)
-    all_copy(link_recv, 5).wait_recv()
-    for owner in range(N_XY):
-        link_table[owner * 4 : owner * 4 + 4, :] = link_recv[owner]
-    codes = jnp.transpose(link_table[...])[0:16]
-    second_half = jnp.where(codes >= 256.0, 1.0, 0.0)
-    codes = jnp.concatenate([codes - 256.0 * second_half, second_half], axis=0).astype(BF16)
-    row16 = iota((16, SLOTS), 0)
-
-    def find_border(select, tile, valid, far, place):
-        found = dot(codes, hits16(row128_16, select.astype(F32)))
-        here = row16 == tile
-        row = jnp.sum(jnp.where(here, found[0:16], 0.0), axis=0, keepdims=True)
-        half = jnp.sum(jnp.where(here, found[16:32], 0.0), axis=0, keepdims=True)
-        return jnp.where(valid, row, -1.0), half * 32.0 + (far * 16 + place).astype(F32)
-
-    def mark_borders(g, unused):
-        for k in range(GROUP):
-            c = g * GROUP + k
-            target = targets_ref[c]
-            owner, tile = target >> 12, (target >> 8) & 15
-            y, x = (target >> 4) & 15, target & 15
-            far_x = jnp.where(x == 15, 1, 0)
-            far_y = jnp.where(y == 15, 1, 0)
-            row, place = find_border(owner * 4 + far_x, tile, (x == 0) | (x == 15), far_x, y)
-            across_hits[c] = hits16(row256, row)
-            across_place[c] = place
-            row, place = find_border(owner * 4 + 2 + far_y, tile, (y == 0) | (y == 15), far_y, x)
-            along_hits[c] = hits16(row256, row)
-            along_place[c] = place
-        return unused
-
-    lax.fori_loop(0, CHUNKS // GROUP, mark_borders, 0)
     all_copy(value_recv, 2).wait_recv()
 
     def add_supply(g, total):
@@ -626,6 +642,38 @@
     change_recv[me] = change_send[me]
     for copy in halos:
         copy.wait_send()
+    all_copy(link_recv, 5).wait_recv()
+    for owner in range(N_XY):
+        link_table[owner * 4 : owner * 4 + 4, :] = link_recv[owner]
+    codes = jnp.transpose(link_table[...])[0:16]
+    second_half = jnp.where(codes >= 256.0, 1.0, 0.0)
+    codes = jnp.concatenate([codes - 256.0 * second_half, second_half], axis=0).astype(BF16)
+    row16 = iota((16, SLOTS), 0)
+
+    def find_border(select, tile, valid, far, place):
+        found = dot(codes, hits16(row128_16, select.astype(F32)))
+        here = row16 == tile
+        row = jnp.sum(jnp.where(here, found[0:16], 0.0), axis=0, keepdims=True)
+        half = jnp.sum(jnp.where(here, found[16:32], 0.0), axis=0, keepdims=True)
+        return jnp.where(valid, row, -1.0), half * 32.0 + (far * 16 + place).astype(F32)
+
+    def mark_borders(g, unused):
+        for k in range(GROUP):
+            c = g * GROUP + k
+            target = targets_ref[c]
+            owner, tile = target >> 12, (target >> 8) & 15
+            y, x = (target >> 4) & 15, target & 15
+            far_x = jnp.where(x == 15, 1, 0)
+            far_y = jnp.where(y == 15, 1, 0)
+            row, place = find_border(owner * 4 + far_x, tile, (x == 0) | (x == 15), far_x, y)
+            across_hits[c] = hits16(row256, row)
+            across_place[c] = place
+            row, place = find_border(owner * 4 + 2 + far_y, tile, (y == 0) | (y == 15), far_y, x)
+            along_hits[c] = hits16(row256, row)
+            along_place[c] = place
+        return unused
+
+    lax.fori_loop(0, CHUNKS // GROUP, mark_borders, 0)
     all_copy(edge_recv1, 3).wait_recv()
     table = edge_recv1[...].reshape(256, 128)
     borders = gather_edges(table, link_hits, link_half)
@@ -761,6 +809,7 @@
             pltpu.SemaphoreType.DMA((14,)),
             pltpu.SemaphoreType.DMA((16,)),
             pltpu.SemaphoreType.DMA((16,)),
+            pltpu.SemaphoreType.REGULAR,
             pltpu.SemaphoreType.DMA((6,)),
             pltpu.SemaphoreType.DMA((6,)),
         ],

time: 40.4 us -> 38.3 us (0.948)
  Pallas kernels: 39.6 us -> 37.6 us
    pallas_call x1, Pallas kernels: 38.1 us -> 36 us  [shards(): pl.pallas_call(kernel, out_shape=(whole, cover_shape, jax.ShapeDtypeStruc...]
where the time goes in v4:
time: 38.3 us; the launch traced here: 38.2 us
  Pallas kernels  37.6 us (98%)
  between operations  0.64 us (2%)
    pallas_call x1, Pallas kernels, shards(): pl.pallas_call(kernel, out_shape=(whole, cover_shape, jax.ShapeDtypeStruc...  36 us
    pallas_call x1, Pallas kernels, shards(): pl.pallas_call(add_kernel, out_shape=(whole, cover_shape), in_specs=[vmem...  1.54 us

profile of v4, /device:TPU:8, one launch (start us, length us, event | category | flops | bytes accessed | tf_op | source)
XLA Modules:
  0.0 38.2 jit_solution(9347075561554785589)
XLA Ops:
  0.6 36.0 %shard_map.86 = (f32[19,8,32,128]{3,2,1,0:T(8,128)S(1)}, f32[16,256]{1,0:T(8,128)S(1)}, f32[256,128]{1,0:T(8,128)S(1)}) custom-call(f32[19,8,32,128]{3,2,1,0:T(8,128)} %pop_hbm.1, s32[8,32,128]{2,1,0:T(8,128)} %solid_hbm.1, f32[8,32,128]{2,1,0:T(8,128)} %knudsen_hbm.1, s32[16,1,256]{2,1,0:T(1,128)} %bitcast.3, s32[16,1,256]{2,1,0:T(1,128)} %bitcast.4, ...), custom_call_target="tpu_custom_call" | custom-call | tf_op jit(solution)/shard_map/pallas_call | solution.py:762
  36.7 1.5 %shard_map.87 = (f32[19,8,32,128]{3,2,1,0:T(8,128)}, f32[16,256]{1,0:T(8,128)}) custom-call(f32[19,8,32,128]{3,2,1,0:T(8,128)S(1)} %get-tuple-element.5.read_ref, f32[256,128]{1,0:T(8,128)S(1)} %get-tuple-element.6.correction_ref, f32[16,256]{1,0:T(8,128)S(1)} %get-tuple-element.7.cover_ref), custom_call_target="tpu_custom_call" | custom-call | tf_op jit(solution)/shard_map/pallas_call | solution.py:833

commit v5 on v4

--- a/solution.py
+++ b/solution.py
@@ -47,6 +47,7 @@
 NEAR = 19
 GREETED = NEAR + 6
 GROUP = 8
+BATCH = 16
 GROUPS = N_XY // GROUP
 
 
@@ -81,9 +82,16 @@
 
 
 def partner(me, step):
-    z = (me % 8 + centred(step // 4, 8)) % 8
-    x = (me // 8 + centred(step % 4, 4)) % 4
+    z = lax.rem(lax.rem(me, 8) + centred(step // 4, 8), 8)
+    x = lax.rem(lax.div(me, 8) + centred(step % 4, 4), 4)
     return x * 8 + z
+
+
+def group_partners(me, group):
+    place_z, place_x = lax.rem(me, 8), lax.div(me, 8)
+    z = (lax.rem(place_z + 4 + group, 8), lax.rem(place_z + 11 - group, 8))
+    x = [lax.rem(place_x + centred(k, 4), 4) * 8 for k in range(4)]
+    return [x[k % 4] + z[k // 4] for k in range(8)]
 
 
 def roll(values, shift, axis):
@@ -230,20 +238,15 @@
 
     barrier = pltpu.get_barrier_semaphore()
 
-    def near(i):
-        step = jnp.where(i >= 8, i + 1, i)
-        z = (me % 8 + step // 4 + 6) % 8
-        x = (me // 8 + step % 4) % 4
-        return x * 8 + z
-
     def greet_near(semaphore):
-        def greet(i, unused):
-            pl.semaphore_signal(
-                semaphore, inc=1, device_id=(gz, near(i)), device_id_type=MESH
-            )
-            return unused
-
-        lax.fori_loop(0, NEAR, greet, 0)
+        for step_z in (2, 6, 1, 7, 0):
+            z = lax.rem(lax.rem(me, 8) + step_z, 8)
+            for step_x in (2, 1, 3, 0):
+                if (step_z, step_x) != (0, 0):
+                    x = lax.rem(lax.div(me, 8) + step_x, 4)
+                    pl.semaphore_signal(
+                        semaphore, inc=1, device_id=(gz, x * 8 + z), device_id_type=MESH
+                    )
 
     for device in (
         (gz_up, up),
@@ -267,12 +270,18 @@
         ).start()
 
     def send_steps(source_of, target_ref, index, first, last):
-        def send(i, unused):
-            other = partner(me, i)
+        for step in range(first, last):
+            other = partner(me, step)
             send_one(source_of(other), target_ref.at[me], index, other)
-            return unused
-
-        lax.fori_loop(first, last, send, 0)
+
+    def send_half(source, target, index, others, group, half):
+        for other in others[half * 4 : half * 4 + 4 - half]:
+            send_one(source.at[other], target.at[me], index, other)
+        if half == 1:
+
+            @pl.when(group < GROUPS - 1)
+            def _():
+                send_one(source.at[others[-1]], target.at[me], index, others[-1])
 
     def all_copy(ref, index):
         part = ref.at[pl.ds(0, OTHERS)]
@@ -422,8 +431,8 @@
     def fill_slots(g, carry):
         base, table = carry
         lefts, rights = [], []
-        for k in range(GROUP):
-            c = g * GROUP + k
+        for k in range(BATCH):
+            c = g * BATCH + k
             start = pl.multiple_of(c * N_XY, N_XY)
             ranks = ranks_ref[pl.ds(start, N_XY), :] + base
             base = base + totals_ref[pl.ds(start, N_XY), :]
@@ -451,7 +460,7 @@
 
     unused, table = lax.fori_loop(
         0,
-        CHUNKS // GROUP,
+        CHUNKS // BATCH,
         fill_slots,
         (jnp.zeros((N_XY, SLOTS), F32), jnp.zeros((4 * N_XY, SLOTS), F32)),
     )
@@ -543,20 +552,15 @@
     dens_t = jnp.concatenate([high, low], axis=0)
 
     def send_values(g, unused):
-        others = [partner(me, g * GROUP + k) for k in range(GROUP)]
-        for other in others:
-            found = dot(dens_t, xy_hits[other])
-            both = found[0:128] + found[128:256]
-            value_send[other] = jnp.sum(
-                jnp.where(row128 == slot_z[other], both, 0.0), axis=0, keepdims=True
-            )
-        send_steps(
-            lambda other: value_send.at[other],
-            value_recv,
-            2,
-            g * GROUP,
-            jnp.minimum(g * GROUP + GROUP, OTHERS),
-        )
+        others = group_partners(me, g)
+        for half in range(2):
+            for other in others[half * 4 : half * 4 + 4]:
+                found = dot(dens_t, xy_hits[other])
+                both = found[0:128] + found[128:256]
+                value_send[other] = jnp.sum(
+                    jnp.where(row128 == slot_z[other], both, 0.0), axis=0, keepdims=True
+                )
+            send_half(value_send, value_recv, 2, others, g, half)
         return unused
 
     lax.fori_loop(0, GROUPS, send_values, 0)
@@ -591,8 +595,8 @@
 
     def add_supply(g, total):
         lefts, rights = [], []
-        for k in range(GROUP):
-            brick = g * GROUP + k
+        for k in range(16):
+            brick = g * 16 + k
             value = value_recv[brick]
             here = row32 == place_row[brick]
             high = value.astype(BF16).astype(F32)
@@ -604,7 +608,7 @@
             rights.append(lane_hits[brick])
         return total + dot_nt(jnp.concatenate(lefts, axis=1), jnp.concatenate(rights, axis=1))
 
-    supply = lax.fori_loop(0, GROUPS, add_supply, jnp.zeros((64, 128), F32))
+    supply = lax.fori_loop(0, N_XY // 16, add_supply, jnp.zeros((64, 128), F32))
     supply = supply[0:32] + supply[32:64]
     supply = jnp.concatenate([supply[0:16], supply[16:32]], axis=1)
     source = cover + 0.3 * supply * (1.0 - cover) - 0.2 * cover
@@ -622,20 +626,15 @@
     change = jnp.concatenate([high, low], axis=0)
 
     def send_changes(g, unused):
-        others = [partner(me, g * GROUP + k) for k in range(GROUP)]
-        for other in others:
-            found = dot(change, lane_hits[other])
-            both = found[0:32] + found[32:64]
-            change_send[other] = jnp.sum(
-                jnp.where(row32 == place_row[other], both, 0.0), axis=0, keepdims=True
-            )
-        send_steps(
-            lambda other: change_send.at[other],
-            change_recv,
-            4,
-            g * GROUP,
-            jnp.minimum(g * GROUP + GROUP, OTHERS),
-        )
+        others = group_partners(me, g)
+        for half in range(2):
+            for other in others[half * 4 : half * 4 + 4]:
+                found = dot(change, lane_hits[other])
+                both = found[0:32] + found[32:64]
+                change_send[other] = jnp.sum(
+                    jnp.where(row32 == place_row[other], both, 0.0), axis=0, keepdims=True
+                )
+            send_half(change_send, change_recv, 4, others, g, half)
         return unused
 
     lax.fori_loop(0, GROUPS, send_changes, 0)
@@ -658,8 +657,8 @@
         return jnp.where(valid, row, -1.0), half * 32.0 + (far * 16 + place).astype(F32)
 
     def mark_borders(g, unused):
-        for k in range(GROUP):
-            c = g * GROUP + k
+        for k in range(BATCH):
+            c = g * BATCH + k
             target = targets_ref[c]
             owner, tile = target >> 12, (target >> 8) & 15
             y, x = (target >> 4) & 15, target & 15
@@ -673,21 +672,19 @@
             along_place[c] = place
         return unused
 
-    lax.fori_loop(0, CHUNKS // GROUP, mark_borders, 0)
+    lax.fori_loop(0, CHUNKS // BATCH, mark_borders, 0)
     all_copy(edge_recv1, 3).wait_recv()
     table = edge_recv1[...].reshape(256, 128)
-    borders = gather_edges(table, link_hits, link_half)
-    cover_out[...] = second + dot(borders.astype(BF16), matrix[512:640]) * (2.0 / 9.0)
-    table = jnp.transpose(table)
-    high, low = split(jnp.concatenate([table[0:32], table[64:96]], axis=0))
+    table_t = jnp.transpose(table)
+    high, low = split(jnp.concatenate([table_t[0:32], table_t[64:96]], axis=0))
     across = jnp.concatenate([high, low], axis=0)
-    high, low = split(jnp.concatenate([table[32:64], table[96:128]], axis=0))
+    high, low = split(jnp.concatenate([table_t[32:64], table_t[96:128]], axis=0))
     along = jnp.concatenate([high, low], axis=0)
     row64 = iota((64, SLOTS), 0).astype(F32)
 
     def add_borders(g, unused):
-        for k in range(GROUP):
-            c = g * GROUP + k
+        for k in range(BATCH):
+            c = g * BATCH + k
             found = dot(across, across_hits[c])
             total = jnp.where(row64 == across_place[c], found[0:64] + found[64:128], 0.0)
             found = dot(along, along_hits[c])
@@ -697,7 +694,9 @@
             border_terms[c] = jnp.sum(total, axis=0, keepdims=True) * (-1.0 / 9.0)
         return unused
 
-    lax.fori_loop(0, CHUNKS // GROUP, add_borders, 0)
+    lax.fori_loop(0, CHUNKS // BATCH, add_borders, 0)
+    borders = gather_edges(table, link_hits, link_half)
+    cover_out[...] = second + dot(borders.astype(BF16), matrix[512:640]) * (2.0 / 9.0)
     all_copy(change_recv, 4).wait_recv()
     got = jnp.concatenate([change_recv[owner] for owner in range(N_XY)], axis=0)
     high, low = split(got)
@@ -705,8 +704,8 @@
 
     def add_change(g, total):
         lefts, rights = [], []
-        for k in range(GROUP):
-            c = g * GROUP + k
+        for k in range(BATCH):
+            c = g * BATCH + k
             found = dot(got, rank_hits[c])
             mine = owner_row == (targets_ref[c] >> 12)
             value = jnp.sum(
@@ -723,7 +722,7 @@
             lefts.append(cell_hits[c])
         return total + dot_nt(jnp.concatenate(lefts, axis=1), jnp.concatenate(rights, axis=1))
 
-    correction = lax.fori_loop(0, CHUNKS // GROUP, add_change, jnp.zeros((256, 256), F32))
+    correction = lax.fori_loop(0, CHUNKS // BATCH, add_change, jnp.zeros((256, 256), F32))
     correction_out[...] = correction[:, 0:128] + correction[:, 128:256]
     for ref, index in (
         (edge_recv0, 0),
@@ -741,7 +740,8 @@
     cover_copy.start()
     copies = []
     for x in range(CX):
-        stage[:, x] = read_ref[:, x] + correction_ref[x * NY : (x + 1) * NY, :][None]
+        for part in (pl.ds(0, 10), pl.ds(10, 9)):
+            stage[part, x] = read_ref[part, x] + correction_ref[x * NY : (x + 1) * NY, :][None]
         copies.append(pltpu.make_async_copy(stage.at[:, x], updated_hbm.at[:, x], sem.at[x]))
         copies[-1].start()
     for copy in copies:

time: 38.3 us -> 34.6 us (0.903)
  Pallas kernels: 37.6 us -> 33.9 us
    pallas_call x1, Pallas kernels: 36 us -> 32.3 us  [shards(): pl.pallas_call(kernel, out_shape=(whole, cover_shape, jax.ShapeDtypeStruc...]
where the time goes in v5:
time: 34.6 us; the launch traced here: 34.5 us
  Pallas kernels  33.9 us (98%)
  between operations  0.64 us (2%)
    pallas_call x1, Pallas kernels, shards(): pl.pallas_call(kernel, out_shape=(whole, cover_shape, jax.ShapeDtypeStruc...  32.3 us
    pallas_call x1, Pallas kernels, shards(): pl.pallas_call(add_kernel, out_shape=(whole, cover_shape), in_specs=[vmem...  1.54 us

profile of v5, /device:TPU:8, one launch (start us, length us, event | category | flops | bytes accessed | tf_op | source)
XLA Modules:
  0.0 34.5 jit_solution(14966487807888368547)
XLA Ops:
  0.6 32.3 %shard_map.86 = (f32[19,8,32,128]{3,2,1,0:T(8,128)S(1)}, f32[16,256]{1,0:T(8,128)S(1)}, f32[256,128]{1,0:T(8,128)S(1)}) custom-call(f32[19,8,32,128]{3,2,1,0:T(8,128)} %pop_hbm.1, s32[8,32,128]{2,1,0:T(8,128)} %solid_hbm.1, f32[8,32,128]{2,1,0:T(8,128)} %knudsen_hbm.1, s32[16,1,256]{2,1,0:T(1,128)} %bitcast.3, s32[16,1,256]{2,1,0:T(1,128)} %bitcast.4, ...), custom_call_target="tpu_custom_call" | custom-call | tf_op jit(solution)/shard_map/pallas_call | solution.py:762
  33.0 1.5 %shard_map.87 = (f32[19,8,32,128]{3,2,1,0:T(8,128)}, f32[16,256]{1,0:T(8,128)}) custom-call(f32[19,8,32,128]{3,2,1,0:T(8,128)S(1)} %get-tuple-element.5.read_ref, f32[256,128]{1,0:T(8,128)S(1)} %get-tuple-element.6.correction_ref, f32[16,256]{1,0:T(8,128)S(1)} %get-tuple-element.7.cover_ref), custom_call_target="tpu_custom_call" | custom-call | tf_op jit(solution)/shard_map/pallas_call | solution.py:833

commit v6 on v5

--- a/solution.py
+++ b/solution.py
@@ -113,7 +113,8 @@
 def tile_edges(cover, picker):
     both = jnp.concatenate([cover[0:8], cover[8:16]], axis=1)
     high, low = split(both)
-    return dot(high, picker) + dot(low, picker)
+    twice = jnp.concatenate([picker, picker], axis=0)
+    return dot(jnp.concatenate([high, low], axis=1), twice)
 
 
 def neighbour_matrix():
@@ -148,10 +149,9 @@
     return jnp.concatenate([out_high, out_low], axis=1)
 
 
-def sweep(cover, source, borders, matrix):
+def neighbour_sum(cover, borders, matrix):
     high, low = split(cover)
-    row = jnp.concatenate([high, low, borders.astype(BF16)], axis=1)
-    return (source + 2.0 * dot(row, matrix)) * (1.0 / 9.0)
+    return dot(jnp.concatenate([high, low, borders.astype(BF16)], axis=1), matrix)
 
 
 def kernel(
@@ -227,14 +227,6 @@
     plane_loads[0] = load(pop_hbm.at[:, 0], pop.at[:, 0], 0)
     cell_loads = [load(solid_hbm, solid, 8), load(knudsen_hbm, knudsen, 9)]
     plane_loads[7] = load(pop_hbm.at[:, 7], pop.at[:, 7], 7)
-    for x in range(1, 7):
-        plane_loads[x] = load(pop_hbm.at[:, x], pop.at[:, x], x)
-    wall_loads = [
-        load(cells_hbm, cells_ref, 10),
-        load(targets_hbm, targets_ref, 11),
-        load(cover_hbm, cover_ref, 12),
-        load(links_hbm, links_ref, 13),
-    ]
 
     barrier = pltpu.get_barrier_semaphore()
 
@@ -258,6 +250,14 @@
     ):
         pl.semaphore_signal(barrier, inc=1, device_id=device, device_id_type=MESH)
     greet_near(barrier)
+    for x in range(1, 7):
+        plane_loads[x] = load(pop_hbm.at[:, x], pop.at[:, x], x)
+    wall_loads = [
+        load(cells_hbm, cells_ref, 10),
+        load(targets_hbm, targets_ref, 11),
+        load(cover_hbm, cover_ref, 12),
+        load(links_hbm, links_ref, 13),
+    ]
 
     def send_one(source, target, index, other):
         pltpu.make_async_remote_copy(
@@ -453,7 +453,6 @@
                 ).astype(BF16)
             )
             rank_hits[c] = hits16(row256, rank)
-            cell_hits[c] = hits16(row256, fields[0].astype(F32))
             rights.append(rank_hits[c])
         table = table + dot_nt(jnp.concatenate(lefts, axis=1), jnp.concatenate(rights, axis=1))
         return base, table
@@ -514,7 +513,7 @@
     send_steps(lambda other: place_send.at[other], place_recv, 1, 0, OTHERS)
     send_steps(lambda other: edge_send0, edge_recv0, 0, 0, OTHERS)
 
-    for copy in halos:
+    for copy in halos[:4] + faces:
         copy.wait_recv()
 
     def finish_plane(i, unused):
@@ -546,6 +545,8 @@
         return unused
 
     lax.fori_loop(1, CX - 1, mend_plane, 0)
+    for copy in halos[4:14]:
+        copy.wait_recv()
     lax.fori_loop(0, 2, finish_plane, 0)
 
     high, low = split(jnp.transpose(dens[...]))
@@ -591,6 +592,7 @@
         return unused
 
     lax.fori_loop(0, GROUPS, mark_places, 0)
+    spread = 2.0 * neighbour_sum(cover, borders, matrix) + 0.8 * cover
     all_copy(value_recv, 2).wait_recv()
 
     def add_supply(g, total):
@@ -611,15 +613,15 @@
     supply = lax.fori_loop(0, N_XY // 16, add_supply, jnp.zeros((64, 128), F32))
     supply = supply[0:32] + supply[32:64]
     supply = jnp.concatenate([supply[0:16], supply[16:32]], axis=1)
-    source = cover + 0.3 * supply * (1.0 - cover) - 0.2 * cover
-    first = sweep(cover, source, borders, matrix)
+    gained = 0.3 * supply * (1.0 - cover)
+    first = (gained + spread) * (1.0 / 9.0)
     edges = tile_edges(first, picker)
     edge_send1[...] = edges
     edge_recv1[me] = edges
     send_steps(lambda other: edge_send1, edge_recv1, 3, 0, OTHERS)
     high, low = split(first)
     second = dot(jnp.concatenate([high, low], axis=1), matrix[0:512])
-    second = (source + 2.0 * second) * (1.0 / 9.0)
+    second = (gained + 0.8 * cover + 2.0 * second) * (1.0 / 9.0)
     change = -0.5 * (second - cover)
     change = jnp.concatenate([change[:, 0:128], change[:, 128:256]], axis=0)
     high, low = split(change)
@@ -661,6 +663,7 @@
             c = g * BATCH + k
             target = targets_ref[c]
             owner, tile = target >> 12, (target >> 8) & 15
+            cell_hits[c] = hits16(row256, (cells_ref[c] >> 7).astype(F32))
             y, x = (target >> 4) & 15, target & 15
             far_x = jnp.where(x == 15, 1, 0)
             far_y = jnp.where(y == 15, 1, 0)

time: 34.6 us -> 34.2 us (0.988)
  Pallas kernels: 33.9 us -> 33.5 us
    pallas_call x1, Pallas kernels: 32.3 us -> 32 us  [shards(): pl.pallas_call(kernel, out_shape=(whole, cover_shape, jax.ShapeDtypeStruc...]
where the time goes in v6:
time: 34.2 us; the launch traced here: 34.1 us
  Pallas kernels  33.5 us (98%)
  between operations  0.64 us (2%)
    pallas_call x1, Pallas kernels, shards(): pl.pallas_call(kernel, out_shape=(whole, cover_shape, jax.ShapeDtypeStruc...  32 us
    pallas_call x1, Pallas kernels, shards(): pl.pallas_call(add_kernel, out_shape=(whole, cover_shape), in_specs=[vmem...  1.54 us

profile of v6, /device:TPU:8, one launch (start us, length us, event | category | flops | bytes accessed | tf_op | source)
XLA Modules:
  0.0 34.1 jit_solution(12452803588470091856)
XLA Ops:
  0.6 32.0 %shard_map.86 = (f32[19,8,32,128]{3,2,1,0:T(8,128)S(1)}, f32[16,256]{1,0:T(8,128)S(1)}, f32[256,128]{1,0:T(8,128)S(1)}) custom-call(f32[19,8,32,128]{3,2,1,0:T(8,128)} %pop_hbm.1, s32[8,32,128]{2,1,0:T(8,128)} %solid_hbm.1, f32[8,32,128]{2,1,0:T(8,128)} %knudsen_hbm.1, s32[16,1,256]{2,1,0:T(1,128)} %bitcast.3, s32[16,1,256]{2,1,0:T(1,128)} %bitcast.4, ...), custom_call_target="tpu_custom_call" | custom-call | tf_op jit(solution)/shard_map/pallas_call | solution.py:765
  32.6 1.5 %shard_map.87 = (f32[19,8,32,128]{3,2,1,0:T(8,128)}, f32[16,256]{1,0:T(8,128)}) custom-call(f32[19,8,32,128]{3,2,1,0:T(8,128)S(1)} %get-tuple-element.5.read_ref, f32[256,128]{1,0:T(8,128)S(1)} %get-tuple-element.6.correction_ref, f32[16,256]{1,0:T(8,128)S(1)} %get-tuple-element.7.cover_ref), custom_call_target="tpu_custom_call" | custom-call | tf_op jit(solution)/shard_map/pallas_call | solution.py:836

commit v7 on v6

--- a/solution.py
+++ b/solution.py
@@ -618,7 +618,7 @@
     edges = tile_edges(first, picker)
     edge_send1[...] = edges
     edge_recv1[me] = edges
-    send_steps(lambda other: edge_send1, edge_recv1, 3, 0, OTHERS)
+    send_steps(lambda other: edge_send1, edge_recv1, 3, 0, 16)
     high, low = split(first)
     second = dot(jnp.concatenate([high, low], axis=1), matrix[0:512])
     second = (gained + 0.8 * cover + 2.0 * second) * (1.0 / 9.0)
@@ -639,7 +639,9 @@
             send_half(change_send, change_recv, 4, others, g, half)
         return unused
 
-    lax.fori_loop(0, GROUPS, send_changes, 0)
+    lax.fori_loop(0, 1, send_changes, 0)
+    send_steps(lambda other: edge_send1, edge_recv1, 3, 16, OTHERS)
+    lax.fori_loop(1, GROUPS, send_changes, 0)
     change_recv[me] = change_send[me]
     for copy in halos:
         copy.wait_send()

time: 34.2 us -> 34.1 us (level)
  no operation moved by 1% of the time
where the time goes in v7:
time: 34.1 us; the launch traced here: 34 us
  Pallas kernels  33.3 us (98%)
  between operations  0.64 us (2%)
    pallas_call x1, Pallas kernels, shards(): pl.pallas_call(kernel, out_shape=(whole, cover_shape, jax.ShapeDtypeStruc...  31.8 us
    pallas_call x1, Pallas kernels, shards(): pl.pallas_call(add_kernel, out_shape=(whole, cover_shape), in_specs=[vmem...  1.54 us

profile of v7, /device:TPU:8, one launch (start us, length us, event | category | flops | bytes accessed | tf_op | source)
XLA Modules:
  0.0 34.0 jit_solution(17574256779397621909)
XLA Ops:
  0.6 31.8 %shard_map.86 = (f32[19,8,32,128]{3,2,1,0:T(8,128)S(1)}, f32[16,256]{1,0:T(8,128)S(1)}, f32[256,128]{1,0:T(8,128)S(1)}) custom-call(f32[19,8,32,128]{3,2,1,0:T(8,128)} %pop_hbm.1, s32[8,32,128]{2,1,0:T(8,128)} %solid_hbm.1, f32[8,32,128]{2,1,0:T(8,128)} %knudsen_hbm.1, s32[16,1,256]{2,1,0:T(1,128)} %bitcast.3, s32[16,1,256]{2,1,0:T(1,128)} %bitcast.4, ...), custom_call_target="tpu_custom_call" | custom-call | tf_op jit(solution)/shard_map/pallas_call | solution.py:767
  32.4 1.5 %shard_map.87 = (f32[19,8,32,128]{3,2,1,0:T(8,128)}, f32[16,256]{1,0:T(8,128)}) custom-call(f32[19,8,32,128]{3,2,1,0:T(8,128)S(1)} %get-tuple-element.5.read_ref, f32[256,128]{1,0:T(8,128)S(1)} %get-tuple-element.6.correction_ref, f32[16,256]{1,0:T(8,128)S(1)} %get-tuple-element.7.cover_ref), custom_call_target="tpu_custom_call" | custom-call | tf_op jit(solution)/shard_map/pallas_call | solution.py:838
